TPU v7x, 256 devices: a whole 4x4x8 slice. The times are simulated.
256 devices in a mesh: section: 4 (over x), ctx: 16 (over z, core), tp: 4 (over y).
Axes of the slice: x: 4, y: 4, z: 8, core: 2. Of those that a mesh axis runs over, the one named last changes fastest.
Arguments:
- hidden_in: bfloat16 [4, 4096, 8192], P('section', 'ctx', 'tp'), may hold values from -6 to 6
- gate_in: bfloat16 [4, 2, 4096, 8192], P('section', None, 'ctx', 'tp'), may hold values from -8 to 8
- state_proj: bfloat16 [4, 2, 2, 4096, 512], P('section', None, None, 'ctx', 'tp'), may hold values from -6 to 6
- step_size: float32 [4, 2, 128, 4096], P('section', None, 'tp', 'ctx'), may hold values from 0.01 to 0.1
- log_decay: float32 [4, 2, 128, 4096], P('section', None, 'tp', 'ctx'), may hold values from -1 to 0
- request_ids: int32 [4, 4096], P('section', 'ctx'), may hold values from 0 to 3, never falling along the last dimension, each value on 1 to 2048 neighbouring positions
- conv_inner: float32 [4, 2, 4, 8192], P('section', None, None, 'tp'), may hold values from -3 to 3
- conv_state: float32 [4, 2, 4, 2, 512], P('section', None, None, None, 'tp'), may hold values from -3 to 3
- skip_gain: float32 [4, 2, 128], P('section', None, 'tp'), may hold values from 0.5 to 2
- norm_gain: float32 [4, 2, 8192], P('section', None, 'tp'), may hold values from 0.5 to 1.5
Outputs:
- hidden_out: bfloat16 [4, 4096, 8192], P('section', 'ctx', 'tp')
Inputs may be any that keep to these rules, and one draw needn't show every extreme that they name: `request_ids`: request numbers never fall along the tokens of a section; each request covers 1 to 2048 tokens, and one covers exactly 2048.
All inputs are finite; a program needn't handle non-finite values.
Results may differ from a plain program's by a relative error of at most 0.007.
Values may be sent and summed in bfloat16 or wider, within the bound.
A program may use at most 128 MiB of HBM per device.

v0:
```python
import jax
import jax.numpy as jnp
from jax import lax
from jax.sharding import PartitionSpec as P

HEADS = 128
HDIM = 64
STATE = 128
KCONV = 4
BLK = 128
MIXER_LAYERS = 2


def passed_along(block, axis, distance):
    devices = range(lax.axis_size(axis))
    route = [(i - distance, i) for i in devices if i - distance in devices]
    return lax.ppermute(block, axis, route)


def prefix_2(part, axis, combine, identity):
    place = lax.axis_index(axis)
    gathered = jax.tree.map(lambda a: lax.all_gather(a, axis), part)
    state = jax.tree.map(lambda a, e: jnp.zeros_like(a) + jnp.asarray(e, a.dtype), part, identity)

    def one(hop, state):
        return combine(
            state, jax.tree.map(lambda a: lax.dynamic_index_in_dim(a, hop, 0, False), gathered)
        )

    return lax.fori_loop(0, place, one, state)


def shifted(block, axis, distance):
    devices = range(lax.axis_size(axis))
    route = [((i - distance) % len(devices), i) for i in devices]
    return lax.ppermute(block, axis, route)


def causal_conv(extended, ext_markers, markers, weights, count):
    summed = jnp.zeros(extended.shape[:-2] + (count, extended.shape[-1]), jnp.float32)
    for tap_idx in range(weights.shape[0]):
        window = lax.slice_in_dim(extended, tap_idx, tap_idx + count, axis=extended.ndim - 2)
        same_req = (ext_markers[tap_idx : tap_idx + count] == markers)[:, None]
        summed = summed + jnp.where(same_req, weights[tap_idx] * window, 0.0)
    return jax.nn.silu(summed).astype(jnp.bfloat16)


def combine_parts(earlier, later_part):
    decay_one, state_one, mark_one = earlier
    decay_two, state_two, mark_two = later_part
    joined = (mark_one == mark_two) | (mark_one == 0.0) | (mark_two == 0.0)
    decay_out = jnp.where(joined, decay_one * decay_two, 0.0)
    state_out = jnp.where(joined, decay_two[:, None, None] * state_one, 0.0) + state_two
    mark_out = jnp.where(mark_two == 0.0, mark_one, mark_two)
    return (decay_out, state_out, mark_out)


def mixer_local(
    stream, gate_rows, proj_rows, step_rows, decay_rows, conv_w, conv_s, skip_w, gain_w, markers
):
    tok_rows = stream.shape[0]
    chan_dev = stream.shape[1]
    head_dev = chan_dev // HDIM
    group_dev = proj_rows.shape[2] // STATE
    head_group = head_dev // group_dev
    block_count = tok_rows // BLK
    tail_start = tok_rows - KCONV + 1
    prev_rows, prev_proj, prev_marks = passed_along(
        (
            stream[tail_start:].astype(jnp.float32),
            proj_rows[:, tail_start:].astype(jnp.float32),
            markers[tail_start:],
        ),
        "ctx",
        1,
    )
    ext_markers = jnp.concatenate([prev_marks, markers])
    xs_rows = causal_conv(
        jnp.concatenate([prev_rows, stream.astype(jnp.float32)], 0),
        ext_markers,
        markers,
        conv_w,
        tok_rows,
    )
    bc_rows = causal_conv(
        jnp.concatenate([prev_proj, proj_rows.astype(jnp.float32)], 1),
        ext_markers,
        markers,
        conv_s[:, :, None, :],
        tok_rows,
    )
    dx_rows = (step_rows.T[:, :, None] * xs_rows.reshape(tok_rows, head_dev, HDIM)).astype(
        jnp.bfloat16
    )
    cum_decay = jnp.cumsum(decay_rows.reshape(head_dev, block_count, BLK), axis=-1).transpose(
        1, 0, 2
    )
    b_blocks = bc_rows[0].reshape(block_count, BLK, group_dev, STATE)
    c_blocks = bc_rows[1].reshape(block_count, BLK, group_dev, STATE)
    dx_blocks = dx_rows.reshape(block_count, BLK, group_dev, head_group, HDIM)
    mark_blocks = markers.reshape(block_count, BLK)
    lower = jnp.arange(BLK)[:, None] >= jnp.arange(BLK)[None, :]
    last_cum = cum_decay[:, :, -1]
    last_mark = mark_blocks[:, -1]
    tail_weight = jnp.where(
        (mark_blocks == last_mark[:, None])[:, None, :],
        jnp.exp(last_cum[:, :, None] - cum_decay),
        0.0,
    )
    b_weighted = (
        tail_weight.reshape(block_count, group_dev, head_group, BLK).transpose(0, 3, 1, 2)[
            ..., None
        ]
        * b_blocks[:, :, :, None, :]
    ).astype(jnp.bfloat16)
    block_sum = jnp.einsum(
        "bsghn,bsghp->bghnp", b_weighted, dx_blocks, preferred_element_type=jnp.float32
    ).reshape(block_count, head_dev, STATE, HDIM)
    block_decay = jnp.exp(last_cum)
    block_mark = last_mark[:, None]
    identity = (
        jnp.ones((head_dev,), jnp.float32),
        jnp.zeros((head_dev, STATE, HDIM), jnp.float32),
        jnp.zeros((1,), jnp.float32),
    )

    def fold_block(carried, block_item):
        return (combine_parts(carried, block_item), None)

    element, _ = lax.scan(fold_block, identity, (block_decay, block_sum, block_mark))
    elem_decay, elem_state, elem_mark = element
    prefix = prefix_2((elem_decay, elem_state, elem_mark), "ctx", combine_parts, identity)
    incoming_state = prefix[1]
    incoming_mark = prefix[2]
    scores = jnp.einsum("btgn,bsgn->bgts", c_blocks, b_blocks, preferred_element_type=jnp.float32)
    allowed = lower[None] & (mark_blocks[:, :, None] == mark_blocks[:, None, :])
    gap_log = cum_decay[:, :, :, None] - cum_decay[:, :, None, :]
    decay_mat = jnp.where(allowed[:, None], jnp.exp(jnp.where(allowed[:, None], gap_log, 0.0)), 0.0)
    mix_weight = (
        scores[:, :, None] * decay_mat.reshape(block_count, group_dev, head_group, BLK, BLK)
    ).astype(jnp.bfloat16)
    y_intra = jnp.einsum(
        "bghts,bsghp->btghp", mix_weight, dx_blocks, preferred_element_type=jnp.float32
    )

    def sweep_block(carried, block_item):
        state_now, mark_now = carried
        decay_now, sum_now, mark_blk = block_item
        new_state = (
            jnp.where(mark_blk == mark_now, decay_now[:, None, None] * state_now, 0.0) + sum_now
        )
        return ((new_state, mark_blk), (state_now, mark_now))

    _, (prior_states, prior_marks) = lax.scan(
        sweep_block, (incoming_state, incoming_mark), (block_decay, block_sum, block_mark)
    )
    factor = jnp.where((mark_blocks == prior_marks)[:, None, :], jnp.exp(cum_decay), 0.0)
    y_state = jnp.einsum(
        "btgn,bghnp->btghp",
        c_blocks.astype(jnp.float32),
        prior_states.reshape(block_count, group_dev, head_group, STATE, HDIM),
        precision=lax.Precision.HIGHEST,
    )
    y_state = (
        y_state
        * factor.reshape(block_count, group_dev, head_group, BLK).transpose(0, 3, 1, 2)[..., None]
    )
    y_rows = (y_intra + y_state).reshape(tok_rows, chan_dev) + jnp.repeat(skip_w, HDIM)[
        None, :
    ] * xs_rows.astype(jnp.float32)
    gated = y_rows * jax.nn.silu(gate_rows.astype(jnp.float32))
    summed_sq = lax.psum(jnp.sum(gated * gated, axis=1), "tp")
    mean_sq = summed_sq / (HEADS * HDIM)
    return (
        stream.astype(jnp.float32) + gated * gain_w[None, :] * lax.rsqrt(mean_sq + 1e-05)[:, None]
    ).astype(jnp.bfloat16)


def per_device(
    hidden_in,
    gate_in,
    state_proj,
    step_size,
    log_decay,
    request_ids,
    conv_inner,
    conv_state,
    skip_gain,
    norm_gain,
):
    markers = (request_ids[0] + 1).astype(jnp.float32)
    stream = hidden_in[0]
    for layer_idx in range(MIXER_LAYERS):
        stream = mixer_local(
            stream,
            gate_in[0, layer_idx],
            state_proj[0, layer_idx],
            step_size[0, layer_idx],
            log_decay[0, layer_idx],
            conv_inner[0, layer_idx],
            conv_state[0, layer_idx],
            skip_gain[0, layer_idx],
            norm_gain[0, layer_idx],
            markers,
        )
    moved = shifted(stream, "section", 1)
    return moved[None]


def solution(mesh):
    in_specs = (
        P("section", "ctx", "tp"),
        P("section", None, "ctx", "tp"),
        P("section", None, None, "ctx", "tp"),
        P("section", None, "tp", "ctx"),
        P("section", None, "tp", "ctx"),
        P("section", "ctx"),
        P("section", None, None, "tp"),
        P("section", None, None, None, "tp"),
        P("section", None, "tp"),
        P("section", None, "tp"),
    )
    out_specs = P("section", "ctx", "tp")
    return jax.shard_map(
        per_device, mesh=mesh, in_specs=in_specs, out_specs=out_specs, check_vma=False
    )
```

profile of v0, /device:TPU:224, one launch (start us, length us, event | category | flops | bytes accessed | tf_op | source)
XLA Modules:
  0.0 600.7 jit_solution(4984952006579031781)
XLA Ops:
  35.1 8.2 %fusion.62 = f32[256,2048]{0,1:T(8,128)} fusion(f32[256,2048]{0,1:T(8,128)} %bitcast_convert_fusion, f32[2048]{0:T(1024)} %bitcast.302, pred[256]{0:T(512)(128)(4,1)} %copy-done.38, f32[3,2048]{0,1:T(8,128)S(1)} %copy.105, f32[2048]{0:T(1024)} %bitcast.303, pred[256]{0:T(512)(128)(4,1)} %copy-done.34, f32[2048]{0:T(1024)} %bitcast.304, ...), kind=kLoop, calls=%fused_computation.121 | loop fusion | flops 10485760 | bytes 4252672 | tf_op jit(solution)/shard_map/convert_element_type | solution.py:92
  43.3 3.3 reshape.315
  46.6 5.2 fusion.38
  51.8 9.2 %while.94 = (s32[]{:T(128)}, f32[32]{0:T(128)S(1)}, f32[32,128,64]{2,1,0:T(8,128)S(1)}, f32[1]{0:T(128)}, f32[2,1]{0,1:T(1,128)S(1)}, /*index=5*/f32[2,32]{1,0:T...) while((s32[]{:T(128)}, f32[32]{0:T(128)S(1)}, ...), condition=%wide.region_2.3_spmd.clone, body=%wide.region_1.2_spmd.clone.sunk | while | flops 1048681 | bytes 3146548 | solution.py:130
  53.7 2.0 bitcast_add_fusion.18
  58.4 2.0 bitcast_add_fusion.18
  66.5 2.7 fusion.99
  79.7 23.1 %all-reduce.5 = (f32[16]{0:T(128)S(1)}, f32[512]{0:T(512)S(1)}) all-reduce(f32[16]{0:T(128)S(1)} %dynamic-update-slice, f32[512]{0:T(512)S(1)} %dynamic-update-slice.1), channel_id=2, replica_groups=mesh['section'=4,'ctx'=16,'tp'=4] {'ctx'}, use_global_device_ids=true, to_apply=%add | all-reduce | flops 528 | bytes 4224
  102.8 4.3 fusion.10
  107.1 51.8 %all-gather.9.cloned.1.call-done = f32[512,128,64]{1,2,0:T(8,128)} async-done(((f32[32,128,64]{1,2,0:T(8,128)}), f32[512,128,64]{1,2,0:T(8,128)}) %all-gather.9.cloned.1.call-update) | async-done | bytes 16777232 | tf_op jit(solution)/shard_map/all_gather | solution.py:22
  159.2 112.6 %while.90 = (s32[]{:T(128)}, f32[32,128,64]{2,1,0:T(8,128)S(1)}, f32[1]{0:T(128)}, s32[]{:T(128)}, f32[16,1]{0,1:T(1,128)S(1)}, /*index=5*/f32[16,32]{1,0:T(8,12...) while((s32[]{:T(128)}, f32[32,128,64]{2,1,0:T(8,128)S(1)}, ...), condition=%wide.region_4.5_spmd, body=%wide.region_3.4_spmd.sunk | while | flops 786443 | bytes 7340626 | solution.py:30
  242.8 2.0 copy.164
  271.8 2.5 broadcast.191.clone
  274.3 10.5 %while.91 = (s32[]{:T(128)}, f32[32,128,64]{2,1,0:T(8,128)S(1)}, f32[1]{0:T(128)}, f32[2,32,128,64]{3,2,1,0:T(8,128)}, f32[2,1]{0,1:T(1,128)S(1)}, /*index=5*/f3...) while((s32[]{:T(128)}, f32[32,128,64]{2,1,0:T(8,128)S(1)}, ...), condition=%wide.region_6.7_spmd, body=%wide.region_5.6_spmd.sunk | while | flops 786435 | bytes 14681139 | solution.py:154
  284.8 6.3 %fusion.45 = f32[2,128,1,32,64]{1,4,3,0,2:T(8,128)S(1)} fusion(f32[2,32,64,128]{3,2,1,0:T(8,128)} %fusion.10, f32[2,32,128,64]{3,2,1,0:T(8,128)} %get-tuple-element.292, bf16[2,128,128,1]{2,1,3,0:T(8,128)(2,1)S(1)} %bitcast.280, f32[2,128,32]{1,2,0:T(8,128)S(1)} %select_bitcast_fusion.2), kind=kOutput, calls=%fused_computation.95 | convolution fusion | flops 806354944 | bytes 6389760 | tf_op jit(solution)/shard_map/btgn,bghnp->btghp/dot_general | solution.py:158
  293.8 10.5 %psum.14 = f32[256]{0:T(256)S(1)} all-reduce(f32[256]{0:T(256)S(1)} %get-tuple-element.627), channel_id=1, replica_groups=mesh['section'=4,'ctx'=16,'tp'=4] {'tp'}, use_global_device_ids=true, to_apply=%region_8.9 | all-reduce | flops 256 | bytes 2048 | tf_op jit(solution)/shard_map/psum | solution.py:172
  307.5 8.4 %collective-permute-start.3 = (f32[3,2048]{1,0:T(4,128)S(1)}, f32[3,2048]{1,0:T(4,128)S(1)}, u32[]{:S(2)}, u32[]{:S(2)}) collective-permute-start(f32[3,2048]{1,0:T(4,128)S(1)} %convert_element_type.193), channel_id=1, source_target_pairs={{0,4},{4,8},{8,12},{12,16},{16,20},{20,24},{24,28},{28,32},{32,36}... | collective-permute-start | bytes 73736 | tf_op jit(solution)/shard_map/ppermute | solution.py:17
  316.9 7.1 %fusion.63 = f32[256,2048]{0,1:T(8,128)S(1)} fusion(f32[256,2048]{0,1:T(8,128)} %get-tuple-element.625, f32[2048]{0:T(1024)S(1)} %bitcast.300, pred[256]{0:T(512)(128)(4,1)S(1)} %copy-done.39, f32[3,2048]{0,1:T(8,128)S(1)} %copy.119, f32[2048]{0:T(1024)S(1)} %bitcast.301, pred[256]{0:T(512)(128)(4,1)S(1)} %copy-done.35, f32[2048]{0:T(1024)S(1)} %bitcast.299, ...), kind=kLoop, calls=%fused_computation.122 | loop fusion | flops 10485760 | bytes 4252672 | tf_op jit(solution)/shard_map/convert_element_type | solution.py:92
  324.1 2.1 reshape.317
  326.2 5.3 fusion.39
  331.5 9.2 %while.95 = (s32[]{:T(128)}, f32[32]{0:T(128)S(1)}, f32[32,128,64]{2,1,0:T(8,128)S(1)}, f32[1]{0:T(128)}, f32[2,1]{0,1:T(1,128)S(1)}, /*index=5*/f32[2,32]{1,0:T...) while((s32[]{:T(128)}, f32[32]{0:T(128)S(1)}, ...), condition=%wide.region_11.12_spmd.clone, body=%wide.region_10.11_spmd.clone.sunk | while | flops 1048681 | bytes 3146548 | solution.py:130
  333.4 2.0 bitcast_add_fusion.19
  338.0 2.0 bitcast_add_fusion.19
  345.1 23.5 %all-reduce.4 = (f32[16]{0:T(128)S(1)}, f32[512]{0:T(512)S(1)}) all-reduce(f32[16]{0:T(128)S(1)} %dynamic-update-slice.2, f32[512]{0:T(512)S(1)} %dynamic-update-slice.3), channel_id=5, replica_groups=mesh['section'=4,'ctx'=16,'tp'=4] {'ctx'}, use_global_device_ids=true, to_apply=%add.2 | all-reduce | flops 528 | bytes 4224
  368.7 3.4 fusion.11
  372.0 61.0 %all-gather.11.cloned.1.call-done = f32[512,128,64]{1,2,0:T(8,128)} async-done(((f32[32,128,64]{1,2,0:T(8,128)}), f32[512,128,64]{1,2,0:T(8,128)}) %all-gather.11.cloned.1.call-update) | async-done | bytes 16777232 | tf_op jit(solution)/shard_map/all_gather | solution.py:22
  433.2 103.9 %while.92 = (s32[]{:T(128)}, f32[32,128,64]{2,1,0:T(8,128)S(1)}, f32[1]{0:T(128)}, s32[]{:T(128)}, f32[16,1]{0,1:T(1,128)S(1)}, /*index=5*/f32[16,32]{1,0:T(8,12...) while((s32[]{:T(128)}, f32[32,128,64]{2,1,0:T(8,128)S(1)}, ...), condition=%wide.region_13.14_spmd, body=%wide.region_12.13_spmd.sunk | while | flops 786443 | bytes 7340626 | solution.py:30
  537.2 2.5 broadcast.191
  539.7 10.9 %while.93 = (s32[]{:T(128)}, f32[32,128,64]{2,1,0:T(8,128)S(1)}, f32[1]{0:T(128)}, f32[2,32,128,64]{3,2,1,0:T(8,128)}, f32[2,1]{0,1:T(1,128)S(1)}, /*index=5*/f3...) while((s32[]{:T(128)}, f32[32,128,64]{2,1,0:T(8,128)S(1)}, ...), condition=%wide.region_15.16_spmd, body=%wide.region_14.15_spmd.sunk | while | flops 786435 | bytes 14681139 | solution.py:154
  550.6 6.3 %fusion.44 = f32[2,128,1,32,64]{1,4,3,0,2:T(8,128)S(1)} fusion(f32[2,32,64,128]{3,2,1,0:T(8,128)} %fusion.11, f32[2,32,128,64]{3,2,1,0:T(8,128)} %get-tuple-element.299, bf16[2,128,128,1]{2,1,3,0:T(8,128)(2,1)S(1)} %bitcast.282, f32[2,128,32]{1,2,0:T(8,128)S(1)} %select_bitcast_fusion), kind=kOutput, calls=%fused_computation.93 | convolution fusion | flops 806354944 | bytes 6389760 | tf_op jit(solution)/shard_map/btgn,bghnp->btghp/dot_general | solution.py:158
  559.6 10.4 %psum.15 = f32[256]{0:T(256)S(1)} all-reduce(f32[256]{0:T(256)S(1)} %get-tuple-element.623), channel_id=1, replica_groups=mesh['section'=4,'ctx'=16,'tp'=4] {'tp'}, use_global_device_ids=true, to_apply=%region_17.18 | all-reduce | flops 256 | bytes 2048 | tf_op jit(solution)/shard_map/psum | solution.py:172
  572.0 20.4 %collective-permute-done.5 = bf16[256,2048]{0,1:T(8,128)(2,1)S(1)} collective-permute-done((bf16[256,2048]{0,1:T(8,128)(2,1)S(1)}, bf16[256,2048]{0,1:T(8,128)(2,1)S(1)}, u32[]{:S(2)}, u32[]{:S(2)}) %collective-permute-start.5) | collective-permute-done | bytes 1048608 | tf_op jit(solution)/shard_map/ppermute | solution.py:36
  (374 shorter events, 240.6 us)
Async XLA Ops:
  6.5 12.4 %copy-start.48 = (f32[1,2,4,2,128]{4,3,2,1,0:T(2,128)S(1)}, f32[1,2,4,2,128]{4,3,2,1,0:T(2,128)}, u32[]{:S(2)}) copy-start(f32[1,2,4,2,128]{4,3,2,1,0:T(2,128)} %param.29) | copy-start | bytes 24580
  6.5 13.1 %copy-start.25 = (f32[1,2,4,2048]{3,2,1,0:T(4,128)S(1)}, f32[1,2,4,2048]{3,2,1,0:T(4,128)}, u32[]{:S(2)}) copy-start(f32[1,2,4,2048]{3,2,1,0:T(4,128)} %param.28) | copy-start | bytes 196612
  6.5 152.4 %all-gather.9.cloned.1.call-start = ((), (), s32[]{:S(2)}) async-start(), calls=%async_computation | async-start | bytes 17825792 | tf_op jit(solution)/shard_map/all_gather | solution.py:22
  7.9 22.3 %collective-permute-start = (f32[3]{0:T(128)}, f32[3]{0:T(128)}, u32[]{:S(2)}, u32[]{:S(2)}) collective-permute-start(f32[3]{0:T(128)} %slice_bitcast_fusion.12), channel_id=1, source_target_pairs={{0,4},{4,8},{8,12},{12,16},{16,20},{20,24},{24,28},{28,32},{32,36}... | collective-permute-start | bytes 44 | tf_op jit(solution)/shard_map/ppermute | solution.py:17
  12.2 18.8 %collective-permute-start.2 = (f32[2,3,128]{2,1,0:T(4,128)}, f32[2,3,128]{2,1,0:T(4,128)}, u32[]{:S(2)}, u32[]{:S(2)}) collective-permute-start(f32[2,3,128]{2,1,0:T(4,128)} %slice_convert_fusion.1), channel_id=1, source_target_pairs={{0,4},{4,8},{8,12},{12,16},{16,20},{20,24},{24,28},{28,32},{32,36}... | collective-permute-start | bytes 9224 | tf_op jit(solution)/shard_map/ppermute | solution.py:17
  15.5 18.5 %collective-permute-start.1 = (f32[3,2048]{1,0:T(4,128)}, f32[3,2048]{1,0:T(4,128)}, u32[]{:S(2)}, u32[]{:S(2)}) collective-permute-start(f32[3,2048]{1,0:T(4,128)} %bitcast_convert_fusion.1), channel_id=1, source_target_pairs={{0,4},{4,8},{8,12},{12,16},{16,20},{20,24},{24,28},{28,32},{32,36}... | collective-permute-start | bytes 73736 | tf_op jit(solution)/shard_map/ppermute | solution.py:17
  18.9 11.3 %copy-start.6 = (bf16[1,256,2048]{1,2,0:T(8,128)(2,1)}, bf16[1,256,2048]{1,2,0:T(8,128)(2,1)S(1)}, u32[]{:S(2)}) copy-start(bf16[1,256,2048]{1,2,0:T(8,128)(2,1)S(1)} %copy.103) | copy-start | bytes 3145732
  25.4 5.6 copy-start.19
  62.6 370.3 %all-gather.11.cloned.1.call-start = ((), (), s32[]{:S(2)}) async-start(), calls=%async_computation.1 | async-start | bytes 17825792 | tf_op jit(solution)/shard_map/all_gather | solution.py:22
  64.0 12.3 %collective-permute-start.4 = (f32[2,3,128]{2,1,0:T(4,128)}, f32[2,3,128]{2,1,0:T(4,128)}, u32[]{:S(2)}, u32[]{:S(2)}) collective-permute-start(f32[2,3,128]{2,1,0:T(4,128)} %slice_convert_fusion), channel_id=1, source_target_pairs={{0,4},{4,8},{8,12},{12,16},{16,20},{20,24},{24,28},{28,32},{32,36}... | collective-permute-start | bytes 9224 | tf_op jit(solution)/shard_map/ppermute | solution.py:17
  69.2 33.6 %copy-start.8 = (f32[2,128,32,64]{1,0,3,2:T(2,128)S(1)}, f32[2,128,32,64]{1,0,3,2:T(2,128)}, u32[]{:S(2)}) copy-start(f32[2,128,32,64]{1,0,3,2:T(2,128)} %reshape.315) | copy-start | bytes 6291460
  74.7 32.4 %copy-start.32 = (pred[2,128,128]{2,1,0:T(8,128)(4,1)}, pred[2,128,128]{2,1,0:T(8,128)(4,1)S(1)}, u32[]{:S(2)}) copy-start(pred[2,128,128]{2,1,0:T(8,128)(4,1)S(1)} %compare_and_fusion) | copy-start | bytes 98308
  274.3 10.5 %copy-start.20 = (f32[32,2,128]{2,0,1:T(8,128)S(1)}, f32[32,2,128]{2,0,1:T(8,128)}, u32[]{:S(2)}) copy-start(f32[32,2,128]{2,0,1:T(8,128)} %copy-done.19) | copy-start | bytes 98308
  293.0 11.3 %copy-start.7 = (bf16[1,256,2048]{1,2,0:T(8,128)(2,1)S(1)}, bf16[1,256,2048]{1,2,0:T(8,128)(2,1)}, u32[]{:S(2)}) copy-start(bf16[1,256,2048]{1,2,0:T(8,128)(2,1)} %copy-done.6) | copy-start | bytes 3145732
  293.0 11.3 %copy-start.31 = (f32[1,1,2048]{2,1,0:T(1,128)S(1)}, f32[1,1,2048]{2,1,0:T(1,128)}, u32[]{:S(2)}) copy-start(f32[1,1,2048]{2,1,0:T(1,128)} %get-tuple-element.652) | copy-start | bytes 24580
  304.3 11.6 %copy-start.15 = (bf16[2,256,128]{2,1,0:T(8,128)(2,1)S(1)}, bf16[2,256,128]{2,1,0:T(8,128)(2,1)}, u32[]{:S(2)}) copy-start(bf16[2,256,128]{2,1,0:T(8,128)(2,1)} %multiply_convert_fusion.10) | copy-start | bytes 393220
  306.1 10.8 %copy-start.26 = (f32[1,1,1,2048]{3,2,1,0:T(1,128)S(1)}, f32[1,1,1,2048]{3,2,1,0:T(1,128)}, u32[]{:S(2)}) copy-start(f32[1,1,1,2048]{3,2,1,0:T(1,128)} %get-tuple-element.644) | copy-start | bytes 24580
  306.1 10.8 %copy-start.27 = (f32[1,1,1,2048]{3,2,1,0:T(1,128)S(1)}, f32[1,1,1,2048]{3,2,1,0:T(1,128)}, u32[]{:S(2)}) copy-start(f32[1,1,1,2048]{3,2,1,0:T(1,128)} %get-tuple-element.649) | copy-start | bytes 24580
  306.1 10.8 %copy-start.28 = (f32[1,1,1,2048]{3,2,1,0:T(1,128)S(1)}, f32[1,1,1,2048]{3,2,1,0:T(1,128)}, u32[]{:S(2)}) copy-start(f32[1,1,1,2048]{3,2,1,0:T(1,128)} %get-tuple-element.650) | copy-start | bytes 24580
  306.1 10.8 %copy-start.35 = (pred[256]{0:T(512)(128)(4,1)S(1)}, pred[256]{0:T(512)(128)(4,1)}, u32[]{:S(2)}) copy-start(pred[256]{0:T(512)(128)(4,1)} %copy-done.34) | copy-start | bytes 772
  306.1 10.8 %copy-start.37 = (pred[256]{0:T(512)(128)(4,1)S(1)}, pred[256]{0:T(512)(128)(4,1)}, u32[]{:S(2)}) copy-start(pred[256]{0:T(512)(128)(4,1)} %copy-done.36) | copy-start | bytes 772
  306.1 10.8 %copy-start.39 = (pred[256]{0:T(512)(128)(4,1)S(1)}, pred[256]{0:T(512)(128)(4,1)}, u32[]{:S(2)}) copy-start(pred[256]{0:T(512)(128)(4,1)} %copy-done.38) | copy-start | bytes 772
  307.5 9.0 %collective-permute-start.3 = (f32[3,2048]{1,0:T(4,128)S(1)}, f32[3,2048]{1,0:T(4,128)S(1)}, u32[]{:S(2)}, u32[]{:S(2)}) collective-permute-start(f32[3,2048]{1,0:T(4,128)S(1)} %convert_element_type.193), channel_id=1, source_target_pairs={{0,4},{4,8},{8,12},{12,16},{16,20},{20,24},{24,28},{28,32},{32,36}... | collective-permute-start | bytes 73736 | tf_op jit(solution)/shard_map/ppermute | solution.py:17
  326.2 5.3 copy-start.2
  326.2 5.3 copy-start.40
  326.2 5.3 copy-start.43
  342.3 26.3 %copy-start.9 = (f32[2,128,32,64]{1,0,3,2:T(2,128)S(1)}, f32[2,128,32,64]{1,0,3,2:T(2,128)}, u32[]{:S(2)}) copy-start(f32[2,128,32,64]{1,0,3,2:T(2,128)} %reshape.317) | copy-start | bytes 6291460
  342.3 26.3 %copy-start.18 = (f32[32,2,128]{2,0,1:T(8,128)S(1)}, f32[32,2,128]{2,0,1:T(8,128)}, u32[]{:S(2)}) copy-start(f32[32,2,128]{2,0,1:T(8,128)} %copy-done.17) | copy-start | bytes 98308
  342.3 26.3 %copy-start.33 = (pred[2,128,128]{2,1,0:T(8,128)(4,1)S(1)}, pred[2,128,128]{2,1,0:T(8,128)(4,1)}, u32[]{:S(2)}) copy-start(pred[2,128,128]{2,1,0:T(8,128)(4,1)} %copy-done.32) | copy-start | bytes 98308
  558.8 11.2 %copy-start.11 = (bf16[256,2048]{0,1:T(8,128)(2,1)S(1)}, bf16[256,2048]{0,1:T(8,128)(2,1)}, u32[]{:S(2)}) copy-start(bf16[256,2048]{0,1:T(8,128)(2,1)} %copy-done.10) | copy-start | bytes 3145732
  558.8 11.2 %copy-start.30 = (f32[1,1,2048]{2,1,0:T(1,128)S(1)}, f32[1,1,2048]{2,1,0:T(1,128)}, u32[]{:S(2)}) copy-start(f32[1,1,2048]{2,1,0:T(1,128)} %get-tuple-element.651) | copy-start | bytes 24580
  570.5 22.0 %collective-permute-start.5 = (bf16[256,2048]{0,1:T(8,128)(2,1)S(1)}, bf16[256,2048]{0,1:T(8,128)(2,1)S(1)}, u32[]{:S(2)}, u32[]{:S(2)}) collective-permute-start(bf16[256,2048]{0,1:T(8,128)(2,1)S(1)} %add_convert_fusion), channel_id=1, source_target_pairs={{192,0},{0,64},{64,128},{128,192},{193,1},{1,65},{65,129},{129,193... | collective-permute-start | bytes 3145736 | tf_op jit(solution)/shard_map/ppermute | solution.py:36
  (30 other events, 78.7 us)
Sparse Core Ops, SparseCore 0:
  62.8 96.1 all-gather.8
  342.5 90.4 all-gather.10
where the time goes:
time: 611 us; the launch traced here: 601 us
  local copies, waits for them, and re-layouts  172 us (28%)
  waiting for transfers between devices  134 us (22%)
  other arithmetic  97 us (16%)
  blocking collectives  67.5 us (11%)
  loops' own time  66.9 us (11%)
  matrix products  31 us (5%)
  starting transfers between devices  17.6 us (3%)
  between operations  14.8 us (2%)
    all_gather x2, waiting for transfers between devices, prefix_2(): gathered = jax.tree.map(lambda a: lax.all_gather(a, axis), part)  113 us
    dynamic_slice x84, local copies, waits for them, and re-layouts, one(): lax.dynamic_index_in_dim(a, hop, 0, False)  109 us
    add x32, other arithmetic, combine_parts(): jnp.where(joined, decay_two[:, None, None] * state_one, 0.0) + state_two  62 us
    another operation x2, loops' own time, prefix_2(): return lax.fori_loop(0, place, one, state)  53.8 us
    unnamed x2, blocking collectives  46.6 us
    psum x2, blocking collectives, mixer_local(): summed_sq = lax.psum(jnp.sum(gated * gated, axis=1), 'tp')  20.9 us
    ppermute x1, waiting for transfers between devices, shifted(): return lax.ppermute(block, axis, route)  20.4 us
    ppermute x5, starting transfers between devices, passed_along(): return lax.ppermute(block, axis, route)  16 us
  transfers between devices with their start and end apart: 8, of which 4 were waited for; matrix products, arithmetic and copies ran while one was open for 7% of the time, Pallas kernels for 0%

commit v1 on v0

v1 whole, which is shorter than its diff:
```python
import functools

import jax
import jax.numpy as jnp
from jax import lax
from jax.experimental import pallas as pl
from jax.experimental.pallas import tpu as pltpu
from jax.sharding import PartitionSpec as P

HDIM = 64
BLK = 128
TOK = 256
CH = 2048
TILE = 256
NT = CH // TILE
HALF = NT // 2
LAYERS = 2
F32 = jnp.float32
BF16 = jnp.bfloat16
MESH = pl.DeviceIdType.MESH


def mm(a, b):
    return jnp.dot(a, b, preferred_element_type=F32)


def mm_nt(a, b):
    return lax.dot_general(a, b, (((1,), (1,)), ((), ())), preferred_element_type=F32)


def iota(shape, dim):
    return lax.broadcasted_iota(jnp.int32, shape, dim)


def parts(v, count):
    out = []
    for _ in range(count - 1):
        p = v.astype(BF16).astype(F32)
        out.append(p)
        v = v - p
    out.append(v)
    return out


def silu_of_half(h):
    return h + h * jnp.tanh(h)


def kernel(
    n_sec,
    n_ctx,
    n_tp,
    hid,
    gate,
    proj,
    step,
    decay,
    ids,
    cw,
    sw,
    skip,
    gain,
    out,
    uext,
    pext,
    idp,
    gbuf,
    mshift,
    e2a,
    e2b,
    e128,
    cts,
    va,
    vb,
    cum_s,
    cmat_s,
    bt_s,
    sc_s,
    xs_s,
    dx_s,
    bs0_s,
    l_s,
    l_r,
    sin_s,
    sout_s,
    x_s,
    xo_s,
    g1,
    g2,
    sq,
    ps_s,
    ps_r,
    r_s,
    in_sem,
    halo_sem,
    first_sem,
    l_sem,
    s_sem,
    x_sem,
    p_sem,
    o_sem,
):
    sec = lax.axis_index("section")
    c = lax.axis_index("ctx")
    tp = lax.axis_index("tp")
    z = lax.div(c, 2)
    k = lax.rem(c, 2)
    last_z = n_ctx // 2 - 1
    partner = c + 1 - 2 * k
    core0 = k == 0

    in_hid = pltpu.make_async_copy(hid.at[0], uext.at[0, pl.ds(BLK, TOK)], in_sem.at[0])
    in_hid.start()
    in_proj = []
    for l in range(LAYERS):
        for w in range(2):
            cp = pltpu.make_async_copy(
                proj.at[0, l, w],
                pext.at[l, pl.ds(BLK, TOK), pl.ds(w * 128, 128)],
                in_sem.at[1 + 2 * l + w],
            )
            cp.start()
            in_proj.append(cp)
    in_gate = [
        pltpu.make_async_copy(gate.at[0, l], gbuf.at[l], in_sem.at[5 + l]) for l in range(LAYERS)
    ]

    @pl.when(c == 0)
    def _():
        for l in range(LAYERS):
            uext[l, pl.ds(112, 16), :] = jnp.zeros((16, CH), BF16)
            pext[l, pl.ds(112, 16), :] = jnp.zeros((16, 256), BF16)
        idp[...] = jnp.full((1, TOK), -1, jnp.int32)

    @pl.when(z == 0)
    def _():
        sin_s[...] = jnp.zeros(sin_s.shape, BF16)

    bar = pltpu.get_barrier_semaphore()

    def greet(**where):
        pl.semaphore_signal(bar, inc=1, device_id=where, device_id_type=MESH)

    @pl.when(c >= 1)
    def _():
        greet(ctx=c - 1)

    @pl.when(c >= 2)
    def _():
        greet(ctx=c - 2)

    @pl.when(core0)
    def _():
        greet(ctx=c + 1)

    for d in range(1, n_tp):
        greet(tp=lax.rem(tp + d, n_tp))
    greet(section=lax.rem(sec + n_sec - 1, n_sec))

    q = iota((128, CH), 0)
    head = iota((128, CH), 1) // HDIM
    e2a[...] = jnp.where((q < 64) & (q % 32 == head), 1.0, 0.0).astype(BF16)
    e2b[...] = jnp.where((q >= 64) & (q % 32 == head), 1.0, 0.0).astype(BF16)
    q = iota((128, 4096), 0)
    head = iota((128, 4096), 1) // 128
    e128[...] = jnp.where((q < 96) & (q % 32 == head), 1.0, 0.0).astype(BF16)
    for l in range(LAYERS):
        uext[l, pl.ds(0, 112), :] = jnp.zeros((112, CH), BF16)
        pext[l, pl.ds(0, 112), :] = jnp.zeros((112, 256), BF16)

    in_hid.wait()
    for cp in in_proj:
        cp.wait()
    for cp in in_gate:
        cp.start()

    greeted = (
        jnp.where(c + 1 < n_ctx, 1, 0) + jnp.where(c + 2 < n_ctx, 1, 0) + k + (n_tp - 1) + 1
    )
    pl.semaphore_wait(bar, greeted)

    def halo_copy(l):
        return pltpu.make_async_remote_copy(
            src_ref=uext.at[l, pl.ds(BLK + TOK - 16, 16)],
            dst_ref=uext.at[l, pl.ds(112, 16)],
            send_sem=halo_sem.at[0, l],
            recv_sem=halo_sem.at[1, l],
            device_id={"ctx": c + 1},
            device_id_type=MESH,
        )

    def first_copies():
        return [
            pltpu.make_async_remote_copy(
                src_ref=ids,
                dst_ref=idp,
                send_sem=first_sem.at[0, 0],
                recv_sem=first_sem.at[1, 0],
                device_id={"ctx": c + 1},
                device_id_type=MESH,
            ),
            pltpu.make_async_remote_copy(
                src_ref=pext.at[:, pl.ds(BLK + TOK - 16, 16)],
                dst_ref=pext.at[:, pl.ds(112, 16)],
                send_sem=first_sem.at[0, 1],
                recv_sem=first_sem.at[1, 1],
                device_id={"ctx": c + 1},
                device_id_type=MESH,
            ),
        ]

    @pl.when(c + 1 < n_ctx)
    def _():
        for cp in first_copies():
            cp.start()
        halo_copy(0).start()

    @pl.when(c >= 1)
    def _():
        for cp in first_copies():
            cp.wait_recv()

    m_row = ids[...].astype(F32)
    m_old = idp[...].astype(F32)
    m_ext = jnp.concatenate([m_old[:, 128:], m_row], axis=1)
    m_prev = m_old[:, 255:256]
    m_e0 = m_row[:, 127:128]
    m_e1 = m_row[:, 255:256]
    m_col = jnp.broadcast_to(m_row, (128, TOK)).T
    for b in range(2):
        mine = m_col[b * BLK : (b + 1) * BLK]
        mine = jnp.concatenate([mine, mine], axis=1)
        same = mine == m_ext[:, b * BLK : b * BLK + 256]
        gap = iota((BLK, 256), 0) + BLK - iota((BLK, 256), 1)
        for j in range(3):
            mshift[b, pl.ds(j * BLK, BLK), :] = jnp.where(same & (gap == j + 1), 1.0, 0.0).astype(
                BF16
            )

    lane = iota((32, TOK), 1)

    def prep(l):
        for b in range(2):
            rows = pl.ds(b * BLK, BLK)
            moved = mm(mshift[b], pext[l, pl.ds(b * BLK, 256), :])
            now = pext[l, pl.ds((b + 1) * BLK, BLK), :].astype(F32)
            taps = [
                0.5 * jnp.concatenate([sw[0, l, t, 0:1, :], sw[0, l, t, 1:2, :]], axis=1)
                for t in range(4)
            ]
            h = taps[3] * now
            for j in range(3):
                h = h + taps[2 - j] * moved[j * BLK : (j + 1) * BLK]
            v = silu_of_half(h)
            bm = v[:, :128]
            cm = v[:, 128:].astype(BF16)
            cmat_s[l, rows, :] = cm
            bt_s[l, :, rows] = bm.T.astype(BF16)
            scores = mm_nt(cm, bm.astype(BF16))
            ok = (iota((BLK, BLK), 0) >= iota((BLK, BLK), 1)) & (
                m_col[b * BLK : (b + 1) * BLK] == m_row[:, b * BLK : (b + 1) * BLK]
            )
            sc_s[l, b] = jnp.where(ok, scores, 0.0)
        d3 = jnp.concatenate(parts(decay[0, l], 3), axis=0).astype(BF16)
        tri = jnp.where(iota((TOK, TOK), 0) <= iota((TOK, TOK), 1), 1.0, 0.0).astype(BF16)
        c3 = mm(d3, tri)
        cum = c3[0:32] + c3[32:64] + c3[64:96]
        for j in range(NT):
            cum_s[l, j, 0:4, :] = cum[4 * j : 4 * j + 4]
        zero = jnp.zeros((32, TOK), F32)
        cts[l] = jnp.concatenate(parts(cum, 3) + [zero], axis=0).T.astype(BF16)
        tot0 = cum[:, 127:128]
        tot1 = cum[:, 255:256]
        first = lane < BLK
        m_e = jnp.where(first[0:1], m_e0, m_e1)
        tail = jnp.where(first, tot0, tot1) - cum
        dt = step[0, l]
        w = dt * jnp.where(m_row == m_e, jnp.exp(jnp.minimum(tail, 0.0)), 0.0)
        va[l] = jnp.concatenate(parts(dt, 2) + parts(w, 2), axis=0).T.astype(BF16)
        f = jnp.where(m_row == m_prev, jnp.exp(jnp.minimum(cum, 0.0)), 0.0)
        f1 = jnp.where(
            (m_row == m_e0) & jnp.logical_not(first), jnp.exp(jnp.minimum(cum - tot0, 0.0)), 0.0
        )
        vb[l] = jnp.concatenate(parts(f, 2) + parts(f1, 2), axis=0).T.astype(BF16)

    prep(0)

    def l_copy(l, i):
        return pltpu.make_async_remote_copy(
            src_ref=l_s.at[l, HALF * (1 - k) + i],
            dst_ref=l_r.at[l, i],
            send_sem=l_sem.at[0, l, i],
            recv_sem=l_sem.at[1, l, i],
            device_id={"ctx": partner},
            device_id_type=MESH,
        )

    def s_copy(l, i):
        return pltpu.make_async_remote_copy(
            src_ref=sout_s.at[l, i],
            dst_ref=sin_s.at[l, i],
            send_sem=s_sem.at[0, l, i],
            recv_sem=s_sem.at[1, l, i],
            device_id={"ctx": c + 2},
            device_id_type=MESH,
        )

    def x_copy(l, i):
        return pltpu.make_async_remote_copy(
            src_ref=xo_s.at[l, i],
            dst_ref=x_s.at[l, HALF * k + i],
            send_sem=x_sem.at[0, l, i],
            recv_sem=x_sem.at[1, l, i],
            device_id={"ctx": partner},
            device_id_type=MESH,
        )

    def x_arrival(l, i):
        return pltpu.make_async_remote_copy(
            src_ref=xo_s.at[l, i],
            dst_ref=x_s.at[l, HALF * (1 - k) + i],
            send_sem=x_sem.at[0, l, i],
            recv_sem=x_sem.at[1, l, i],
            device_id={"ctx": partner},
            device_id_type=MESH,
        )

    def p_copy(l, d):
        return pltpu.make_async_remote_copy(
            src_ref=ps_s.at[l],
            dst_ref=ps_r.at[l, d - 1],
            send_sem=p_sem.at[0, l, d - 1],
            recv_sem=p_sem.at[1, l, d - 1],
            device_id={"tp": lax.rem(tp + d, n_tp)},
            device_id_type=MESH,
        )

    def o_copy(i):
        row = TOK - 32 * (i + 1)
        return pltpu.make_async_remote_copy(
            src_ref=uext.at[LAYERS, pl.ds(pl.multiple_of(BLK + row, 32), 32)],
            dst_ref=out.at[0, pl.ds(pl.multiple_of(row, 32), 32)],
            send_sem=o_sem.at[0, i],
            recv_sem=o_sem.at[1, i],
            device_id={"section": lax.rem(sec + 1, n_sec)},
            device_id_type=MESH,
        )

    def local_part(l, i):
        tile = lax.rem(i + HALF * (1 - k), NT)
        cols = pl.ds(pl.multiple_of(tile * TILE, TILE), TILE)
        taps = [0.5 * cw[0, l, pl.ds(t, 1), cols] for t in range(4)]
        ea, eb = e2a[:, cols], e2b[:, cols]
        sums = []
        for b in range(2):
            rows = pl.ds(b * BLK, BLK)
            moved = mm(mshift[b], uext[l, pl.ds(b * BLK, 256), cols])
            h = taps[3] * uext[l, pl.ds((b + 1) * BLK, BLK), cols].astype(F32)
            for j in range(3):
                h = h + taps[2 - j] * moved[j * BLK : (j + 1) * BLK]
            xs = silu_of_half(h).astype(BF16)
            xs_s[rows, cols] = xs
            xs = xs.astype(F32)
            v = va[l, rows, :]
            dx_s[rows, cols] = (mm(v, ea) * xs).astype(BF16)
            sums.append(mm(bt_s[l, :, rows], (mm(v, eb) * xs).astype(BF16)))
        vend = vb[l, pl.ds(TOK - 16, 16), :]
        d_all = mm(vend, ea)[15:16]
        d_blk = mm(vend, eb)[15:16]
        bs0_s[tile] = sums[0].astype(BF16)
        l_s[l, tile, pl.ds(0, 128), :] = (d_blk * sums[0] + sums[1]).astype(BF16)
        hi, lo = parts(d_all, 2)
        row = iota((16, TILE), 0)
        l_s[l, tile, pl.ds(128, 16), :] = jnp.where(
            row == 0, hi, jnp.where(row == 1, lo, 0.0)
        ).astype(BF16)

    def chain(l, i):
        l_copy(l, i).wait_recv()

        @pl.when(z > 0)
        def _():
            s_copy(l, i).wait_recv()

        tile = HALF * k + i

        def both(ref):
            d = ref[pl.ds(128, 16), :].astype(F32)
            return ref[pl.ds(0, 128), :].astype(F32), d[0:1] + d[1:2]

        mine, d_mine = both(l_s.at[l, tile])
        other, d_other = both(l_r.at[l, i])
        s = sin_s[l, i].astype(F32)
        x1 = jnp.where(core0, mine, other) + jnp.where(core0, d_mine, d_other) * s
        end = jnp.where(core0, other, mine) + jnp.where(core0, d_other, d_mine) * x1
        sout_s[l, i] = end.astype(BF16)

        @pl.when(z < last_z)
        def _():
            s_copy(l, i).start()

        x_s[l, tile] = jnp.where(core0, s, x1).astype(BF16)
        xo_s[l, i] = jnp.where(core0, x1, s).astype(BF16)
        x_copy(l, i).start()

    low = iota((BLK, 128), 1) < HDIM
    low_row = iota((1, 128), 1) < HDIM

    def intra(l, tile):
        cols = pl.ds(pl.multiple_of(tile * TILE, TILE), TILE)
        for b in range(2):
            rows = pl.ds(b * BLK, BLK)
            scores = sc_s[l, b]
            ys = []
            for p in range(2):
                h0 = 4 * tile + 2 * p
                pair = pl.ds(pl.multiple_of(tile * TILE + p * 128, 128), 128)
                ct = mm(
                    cts[l, rows, :],
                    e128[:, pl.ds(pl.multiple_of(tile * 512 + p * 256, 256), 256)],
                )
                mix = []
                for o in range(2):
                    gap = ct[:, o * 128 : (o + 1) * 128] - cum_s[l, tile, 2 * p + o : 2 * p + o + 1, rows]
                    mix.append((scores * jnp.exp(jnp.minimum(gap, 0.0))).astype(BF16))
                dx = dx_s[rows, pair].astype(F32)
                both = jnp.concatenate(
                    [jnp.where(low, dx, 0.0), jnp.where(low, 0.0, dx)], axis=0
                ).astype(BF16)
                y = mm(jnp.concatenate(mix, axis=1), both)
                gains = jnp.where(low_row, skip[0, l, h0], skip[0, l, h0 + 1])
                ys.append(y + gains * xs_s[rows, pair].astype(F32))
            y = jnp.concatenate(ys, axis=1)
            v = vb[l, rows, :]
            if b == 1:
                y = y + mm(v, e2b[:, cols]) * mm(cmat_s[l, rows, :], bs0_s[tile])
            h = 0.5 * gbuf[l, rows, cols].astype(F32)
            sg = silu_of_half(h)
            g1[rows, cols] = y * sg
            g2[rows, cols] = mm(v, e2a[:, cols]) * sg

    def layer(l, carry):
        @pl.when(c >= 1)
        def _():
            halo_copy(l).wait_recv()

        def a_step(i, carry):
            local_part(l, i)

            @pl.when(i < HALF)
            def _():
                l_copy(l, i).start()

            return carry

        lax.fori_loop(0, NT, a_step, 0)

        early = (l == 1) | (z <= 1)

        @pl.when(l == 0)
        def _():
            for cp in in_gate:
                cp.wait()

        def b_step(i, carry):
            @pl.when(early)
            def _():
                chain(l, i)

            intra(l, 2 * i)
            intra(l, 2 * i + 1)
            return carry

        lax.fori_loop(0, HALF, b_step, 0)

        @pl.when(l == 0)
        def _():
            prep(1)

        def c_step(i, carry):
            @pl.when(jnp.logical_not(early))
            def _():
                chain(l, i)

            return carry

        lax.fori_loop(0, HALF, c_step, 0)

        sq[...] = jnp.zeros((TOK, 128), F32)

        def d_step(i, carry):
            @pl.when(i >= HALF)
            def _():
                x_arrival(l, i - HALF).wait_recv()

            tile = lax.rem(i + HALF * k, NT)
            cols = pl.ds(pl.multiple_of(tile * TILE, TILE), TILE)
            g = g1[:, cols] + g2[:, cols] * mm(cmat_s[l], x_s[l, tile])
            g1[:, cols] = g
            g = g * g
            sq[...] += g[:, :128] + g[:, 128:]
            return carry

        lax.fori_loop(0, NT, d_step, 0)

        hi, lo = parts(sq[...], 2)
        ones = jnp.ones((16, 128), BF16)
        total = (mm_nt(ones, hi.astype(BF16)) + mm_nt(ones, lo.astype(BF16)))[0:8]
        ps_s[l] = total
        for d in range(1, n_tp):
            p_copy(l, d).start()
        for d in range(1, n_tp):
            p_copy(l, d).wait_recv()
            total = total + ps_r[l, d - 1]
        scale = lax.rsqrt(total[0:1] / (CH * n_tp) + 1e-05)
        r_s[...] = jnp.broadcast_to(scale, (128, TOK)).T

        def e_step(i, carry):
            row = TOK - 32 * (i + 1)
            rows = pl.ds(pl.multiple_of(row, 32), 32)
            ext = pl.ds(pl.multiple_of(BLK + row, 32), 32)
            r = r_s[rows, :]
            for t in range(CH // 128):
                cols = pl.ds(t * 128, 128)
                gains = jnp.where(l == 0, gain[0, 0:1, cols], gain[0, 1:2, cols])
                uext[l + 1, ext, cols] = (
                    uext[l, ext, cols].astype(F32) + g1[rows, cols] * (gains * r)
                ).astype(BF16)

            @pl.when((l == 0) & (i == 0) & (c + 1 < n_ctx))
            def _():
                halo_copy(1).start()

            @pl.when(l == LAYERS - 1)
            def _():
                o_copy(i).start()

            return carry

        lax.fori_loop(0, TOK // 32, e_step, 0)
        return carry

    lax.fori_loop(0, LAYERS, layer, 0)

    @pl.when(c + 1 < n_ctx)
    def _():
        for cp in first_copies():
            cp.wait_send()
        for l in range(LAYERS):
            halo_copy(l).wait_send()

    def sent(n, carry):
        l, i = n // HALF, lax.rem(n, HALF)
        l_copy(l, i).wait_send()
        x_copy(l, i).wait_send()

        @pl.when(z < last_z)
        def _():
            s_copy(l, i).wait_send()

        return carry

    lax.fori_loop(0, LAYERS * HALF, sent, 0)
    for l in range(LAYERS):
        for d in range(1, n_tp):
            p_copy(l, d).wait_send()

    def moved(i, carry):
        o_copy(i).wait_send()
        o_copy(i).wait_recv()
        return carry

    lax.fori_loop(0, TOK // 32, moved, 0)


def per_device(sizes, *args):
    hbm = pl.BlockSpec(memory_space=pl.ANY)
    vmem = pl.BlockSpec(memory_space=pltpu.VMEM)
    smem = pl.BlockSpec(memory_space=pltpu.SMEM)
    dma = pltpu.SemaphoreType.DMA
    n_tp = sizes[2]
    return pl.pallas_call(
        functools.partial(kernel, *sizes),
        out_shape=jax.ShapeDtypeStruct((1, TOK, CH), BF16),
        in_specs=[hbm, hbm, hbm, vmem, vmem, vmem, vmem, vmem, smem, vmem],
        out_specs=hbm,
        scratch_shapes=[
            pltpu.VMEM((LAYERS + 1, BLK + TOK, CH), BF16),
            pltpu.VMEM((LAYERS, BLK + TOK, 256), BF16),
            pltpu.VMEM((1, TOK), jnp.int32),
            pltpu.VMEM((LAYERS, TOK, CH), BF16),
            pltpu.VMEM((2, 3 * BLK, 256), BF16),
            pltpu.VMEM((128, CH), BF16),
            pltpu.VMEM((128, CH), BF16),
            pltpu.VMEM((128, 4096), BF16),
            pltpu.VMEM((LAYERS, TOK, 128), BF16),
            pltpu.VMEM((LAYERS, TOK, 128), BF16),
            pltpu.VMEM((LAYERS, TOK, 128), BF16),
            pltpu.VMEM((LAYERS, NT, 8, TOK), F32),
            pltpu.VMEM((LAYERS, TOK, 128), BF16),
            pltpu.VMEM((LAYERS, 128, TOK), BF16),
            pltpu.VMEM((LAYERS, 2, BLK, BLK), F32),
            pltpu.VMEM((TOK, CH), BF16),
            pltpu.VMEM((TOK, CH), BF16),
            pltpu.VMEM((NT, 128, TILE), BF16),
            pltpu.VMEM((LAYERS, NT, 144, TILE), BF16),
            pltpu.VMEM((LAYERS, HALF, 144, TILE), BF16),
            pltpu.VMEM((LAYERS, HALF, 128, TILE), BF16),
            pltpu.VMEM((LAYERS, HALF, 128, TILE), BF16),
            pltpu.VMEM((LAYERS, NT, 128, TILE), BF16),
            pltpu.VMEM((LAYERS, HALF, 128, TILE), BF16),
            pltpu.VMEM((TOK, CH), F32),
            pltpu.VMEM((TOK, CH), F32),
            pltpu.VMEM((TOK, 128), F32),
            pltpu.VMEM((LAYERS, 8, TOK), F32),
            pltpu.VMEM((LAYERS, max(n_tp - 1, 1), 8, TOK), F32),
            pltpu.VMEM((TOK, 128), F32),
            dma((7,)),
            dma((2, LAYERS)),
            dma((2, 2)),
            dma((2, LAYERS, HALF)),
            dma((2, LAYERS, HALF)),
            dma((2, LAYERS, HALF)),
            dma((2, LAYERS, max(n_tp - 1, 1))),
            dma((2, TOK // 32)),
        ],
        compiler_params=pltpu.CompilerParams(
            collective_id=0, has_side_effects=True, vmem_limit_bytes=48 * 1024 * 1024
        ),
        cost_estimate=pl.CostEstimate(
            flops=2_000_000_000, bytes_accessed=6_000_000, transcendentals=6_000_000
        ),
        name="mixer",
    )(*args)


def solution(mesh):
    in_specs = (
        P("section", "ctx", "tp"),
        P("section", None, "ctx", "tp"),
        P("section", None, None, "ctx", "tp"),
        P("section", None, "tp", "ctx"),
        P("section", None, "tp", "ctx"),
        P("section", "ctx"),
        P("section", None, None, "tp"),
        P("section", None, None, None, "tp"),
        P("section", None, "tp"),
        P("section", None, "tp"),
    )
    out_specs = P("section", "ctx", "tp")
    sizes = tuple(mesh.shape[a] for a in ("section", "ctx", "tp"))
    return jax.shard_map(
        functools.partial(per_device, sizes),
        mesh=mesh,
        in_specs=in_specs,
        out_specs=out_specs,
        check_vma=False,
    )
```

time: 611 us -> 96.6 us (0.16); the launches traced: 601 us -> 96.2 us
  local copies, waits for them, and re-layouts: 172 us -> 10 us
  waiting for transfers between devices: 134 us -> 0 us
  other arithmetic: 97 us -> 0 us
  Pallas kernels: 0 us -> 86.1 us
  blocking collectives: 67.5 us -> 0 us
  loops' own time: 66.9 us -> 0 us
  matrix products: 31 us -> 0 us
  starting transfers between devices: 17.6 us -> 0 us
  between operations: 14.8 us -> 0.02 us
    dynamic_slice x92 -> x0, local copies, waits for them, and re-layouts: 114 us -> none  [the longest x84 109 us: one(): lax.dynamic_index_in_dim(a, hop, 0, False)]
    all_gather x2 -> x0, waiting for transfers between devices: 113 us -> none  [prefix_2(): gathered = jax.tree.map(lambda a: lax.all_gather(a, axis), part)]
    pallas_call x0 -> x1, Pallas kernels: none -> 86.1 us  [per_device(): pl.pallas_call(functools.partial(kernel, *sizes), out_shape=jax.ShapeDtyp...]
    another operation x6 -> x0, loops' own time: 66.9 us -> none  [the longest x2 53.8 us: prefix_2(): return lax.fori_loop(0, place, one, state)]
    add x36 -> x0, other arithmetic: 63.4 us -> none  [the longest x32 62 us: combine_parts(): jnp.where(joined, decay_two[:, None, None] * state_one, 0.0) + state_two]
    unnamed x2 -> x0, blocking collectives: 46.6 us -> none
    dot_general x8 -> x0, matrix products: 31 us -> none  [the longest x2 12.6 us: mixer_local(): jnp.einsum('btgn,bghnp->btghp', c_blocks.astype(jnp.float32), prior_state...]
    convert_element_type x14 -> x0, other arithmetic: 27 us -> none  [the longest x2 15.3 us: mixer_local(): step_rows.T[:, :, None] * xs_rows.reshape(tok_rows, head_dev, HDIM)]
  transfers between devices with their start and end apart: 8 -> 0, of which waited for: 4 -> 0; matrix products, arithmetic and copies ran while one was open for 7% -> 0% of each run, Pallas kernels for 0% -> 0%
where the time goes in v1:
time: 96.6 us; the launch traced here: 96.2 us
  Pallas kernels  86.1 us (89%)
  local copies, waits for them, and re-layouts  10 us (10%)
    pallas_call x1, Pallas kernels, per_device(): pl.pallas_call(functools.partial(kernel, *sizes), out_shape=jax.ShapeDtyp...  86.1 us
    unnamed x21, local copies, waits for them, and re-layouts  10 us

profile of v1, /device:TPU:224, one launch (start us, length us, event | category | flops | bytes accessed | tf_op | source)
XLA Modules:
  0.0 96.2 jit_solution(6157923378050535010)
XLA Ops:
  0.0 0.0 copy-start
  0.0 1.6 %copy-done = bf16[1,2,256,2048]{3,2,1,0:T(8,128)(2,1)S(1)} copy-done((bf16[1,2,256,2048]{3,2,1,0:T(8,128)(2,1)S(1)}, bf16[1,2,256,2048]{3,2,1,0:T(8,128)(2,1)}, u32[]{:S(2)}) %copy-start) | copy-done | bytes 2097176
  1.6 0.0 copy-start.1
  1.6 1.2 %copy-done.1 = bf16[1,256,2048]{2,1,0:T(8,128)(2,1)S(1)} copy-done((bf16[1,256,2048]{2,1,0:T(8,128)(2,1)S(1)}, bf16[1,256,2048]{2,1,0:T(8,128)(2,1)}, u32[]{:S(2)}) %copy-start.1) | copy-done | bytes 1048600
  2.8 0.0 copy-start.2
  2.8 0.9 copy-done.2
  3.8 0.0 copy-start.3
  3.8 0.8 copy-done.3
  4.6 0.0 copy-start.4
  4.6 0.8 copy-done.4
  5.4 0.0 copy-start.5
  5.5 0.8 copy-done.5
  6.3 0.0 copy-start.6
  6.3 0.7 copy-done.6
  7.0 0.0 copy-start.7
  7.0 0.7 copy-done.7
  7.7 0.0 copy-start.8
  7.7 0.7 copy-done.8
  8.4 0.0 copy-start.9
  8.4 0.7 copy-done.9
  9.1 86.1 %mixer.1 = bf16[1,256,2048]{2,1,0:T(8,128)(2,1)S(1)} custom-call(bf16[1,256,2048]{2,1,0:T(8,128)(2,1)S(1)} %copy-done.1, bf16[1,2,256,2048]{3,2,1,0:T(8,128)(2,1)S(1)} %copy-done, bf16[1,2,2,256,128]{4,3,2,1,0:T(8,128)(2,1)S(1)} %copy-done.2, f32[1,2,32,256]{3,2,1,0:T(8,128)S(1)} %copy-done.3, f32[1,2,32,256]{3,2,1,0:T(8,128)S(1)} %copy-done.4, ...), custom_call_target="tpu_custom_call" | custom-call | flops 2000000000 | bytes 6000000 | tf_op jit(solution)/shard_map/mixer/pallas_call | solution.py:582
  95.2 1.0 %copy.12 = bf16[1,256,2048]{2,1,0:T(8,128)(2,1)} copy(bf16[1,256,2048]{2,1,0:T(8,128)(2,1)S(1)} %mixer.1) | data formatting | bytes 2097152
Async XLA Ops:
  0.0 1.6 %copy-start = (bf16[1,2,256,2048]{3,2,1,0:T(8,128)(2,1)S(1)}, bf16[1,2,256,2048]{3,2,1,0:T(8,128)(2,1)}, u32[]{:S(2)}) copy-start(bf16[1,2,256,2048]{3,2,1,0:T(8,128)(2,1)} %gate.1) | copy-start | bytes 6291460
  1.6 1.2 %copy-start.1 = (bf16[1,256,2048]{2,1,0:T(8,128)(2,1)S(1)}, bf16[1,256,2048]{2,1,0:T(8,128)(2,1)}, u32[]{:S(2)}) copy-start(bf16[1,256,2048]{2,1,0:T(8,128)(2,1)} %hid.1) | copy-start | bytes 3145732
  2.8 0.9 copy-start.2
  3.8 0.8 copy-start.3
  4.6 0.8 copy-start.4
  5.4 0.8 copy-start.5
  6.3 0.7 copy-start.6
  7.0 0.7 copy-start.7
  7.7 0.7 copy-start.8
  8.4 0.7 copy-start.9

commit v2 on v1

--- a/solution.py
+++ b/solution.py
@@ -14,6 +14,10 @@
 TILE = 256
 NT = CH // TILE
 HALF = NT // 2
+HC = 2 * HALF
+RC = TOK // 32
+ROUND = RC // 4
+LAG = 4
 LAYERS = 2
 F32 = jnp.float32
 BF16 = jnp.bfloat16
@@ -53,6 +57,14 @@
     hid,
     gate,
     proj,
+    step_h,
+    decay_h,
+    ids_h,
+    cw_h,
+    sw_h,
+    skip_h,
+    gain_h,
+    out,
     step,
     decay,
     ids,
@@ -60,7 +72,6 @@
     sw,
     skip,
     gain,
-    out,
     uext,
     pext,
     idp,
@@ -99,6 +110,8 @@
     x_sem,
     p_sem,
     o_sem,
+    r_sem,
+    relay,
 ):
     sec = lax.axis_index("section")
     c = lax.axis_index("ctx")
@@ -109,6 +122,21 @@
     partner = c + 1 - 2 * k
     core0 = k == 0
 
+    in_small = []
+    for n, (src, dst) in enumerate(
+        [
+            (ids_h, ids),
+            (decay_h, decay),
+            (step_h, step),
+            (sw_h, sw),
+            (cw_h, cw),
+            (skip_h, skip),
+            (gain_h, gain),
+        ]
+    ):
+        cp = pltpu.make_async_copy(src, dst, in_sem.at[7 + n])
+        cp.start()
+        in_small.append(cp)
     in_hid = pltpu.make_async_copy(hid.at[0], uext.at[0, pl.ds(BLK, TOK)], in_sem.at[0])
     in_hid.start()
     in_proj = []
@@ -156,6 +184,8 @@
     for d in range(1, n_tp):
         greet(tp=lax.rem(tp + d, n_tp))
     greet(section=lax.rem(sec + n_sec - 1, n_sec))
+    if n_sec > 2:
+        greet(section=lax.rem(sec + 1, n_sec))
 
     q = iota((128, CH), 0)
     head = iota((128, CH), 1) // HDIM
@@ -169,13 +199,13 @@
         pext[l, pl.ds(0, 112), :] = jnp.zeros((112, 256), BF16)
 
     in_hid.wait()
-    for cp in in_proj:
+    for cp in in_proj + in_small:
         cp.wait()
     for cp in in_gate:
         cp.start()
 
     greeted = (
-        jnp.where(c + 1 < n_ctx, 1, 0) + jnp.where(c + 2 < n_ctx, 1, 0) + k + (n_tp - 1) + 1
+        jnp.where(c + 1 < n_ctx, 1, 0) + jnp.where(c + 2 < n_ctx, 1, 0) + k + (n_tp - 1) + min(n_sec - 1, 2)
     )
     pl.semaphore_wait(bar, greeted)
 
@@ -305,10 +335,13 @@
             device_id_type=MESH,
         )
 
+    def half_tile(i):
+        return pl.ds(pl.multiple_of(lax.rem(i, 2) * 128, 128), 128)
+
     def x_copy(l, i):
         return pltpu.make_async_remote_copy(
             src_ref=xo_s.at[l, i],
-            dst_ref=x_s.at[l, HALF * k + i],
+            dst_ref=x_s.at[l, HALF * k + lax.div(i, 2), :, half_tile(i)],
             send_sem=x_sem.at[0, l, i],
             recv_sem=x_sem.at[1, l, i],
             device_id={"ctx": partner},
@@ -318,7 +351,7 @@
     def x_arrival(l, i):
         return pltpu.make_async_remote_copy(
             src_ref=xo_s.at[l, i],
-            dst_ref=x_s.at[l, HALF * (1 - k) + i],
+            dst_ref=x_s.at[l, HALF * (1 - k) + lax.div(i, 2), :, half_tile(i)],
             send_sem=x_sem.at[0, l, i],
             recv_sem=x_sem.at[1, l, i],
             device_id={"ctx": partner},
@@ -343,6 +376,17 @@
             send_sem=o_sem.at[0, i],
             recv_sem=o_sem.at[1, i],
             device_id={"section": lax.rem(sec + 1, n_sec)},
+            device_id_type=MESH,
+        )
+
+    def round_copy(i, hop):
+        row = TOK - 32 * (i + 1)
+        return pltpu.make_async_remote_copy(
+            src_ref=uext.at[LAYERS, pl.ds(BLK + row, 32)] if hop == 0 else relay.at[hop - 1, i],
+            dst_ref=out.at[0, pl.ds(row, 32)] if hop == n_sec - 2 else relay.at[hop, i],
+            send_sem=r_sem.at[0, hop, i],
+            recv_sem=r_sem.at[1, hop, i],
+            device_id={"section": lax.rem(sec + n_sec - 1, n_sec)},
             device_id_type=MESH,
         )
 
@@ -376,20 +420,23 @@
         ).astype(BF16)
 
     def chain(l, i):
-        l_copy(l, i).wait_recv()
+        @pl.when(lax.rem(i, 2) == 0)
+        def _():
+            l_copy(l, lax.div(i, 2)).wait_recv()
 
         @pl.when(z > 0)
         def _():
             s_copy(l, i).wait_recv()
 
-        tile = HALF * k + i
+        tile = HALF * k + lax.div(i, 2)
+        lanes = half_tile(i)
 
         def both(ref):
-            d = ref[pl.ds(128, 16), :].astype(F32)
-            return ref[pl.ds(0, 128), :].astype(F32), d[0:1] + d[1:2]
+            d = ref[pl.ds(128, 16), lanes].astype(F32)
+            return ref[pl.ds(0, 128), lanes].astype(F32), d[0:1] + d[1:2]
 
         mine, d_mine = both(l_s.at[l, tile])
-        other, d_other = both(l_r.at[l, i])
+        other, d_other = both(l_r.at[l, lax.div(i, 2)])
         s = sin_s[l, i].astype(F32)
         x1 = jnp.where(core0, mine, other) + jnp.where(core0, d_mine, d_other) * s
         end = jnp.where(core0, other, mine) + jnp.where(core0, d_other, d_mine) * x1
@@ -399,7 +446,7 @@
         def _():
             s_copy(l, i).start()
 
-        x_s[l, tile] = jnp.where(core0, s, x1).astype(BF16)
+        x_s[l, tile, :, lanes] = jnp.where(core0, s, x1).astype(BF16)
         xo_s[l, i] = jnp.where(core0, x1, s).astype(BF16)
         x_copy(l, i).start()
 
@@ -455,43 +502,38 @@
 
         lax.fori_loop(0, NT, a_step, 0)
 
-        early = (l == 1) | (z <= 1)
-
         @pl.when(l == 0)
         def _():
             for cp in in_gate:
                 cp.wait()
 
+        lag = jnp.where(l == 0, jnp.minimum(LAG * z, NT), 0)
+        prep_at = jnp.where(z <= 2, 2 * NT - 1, NT)
+
         def b_step(i, carry):
-            @pl.when(early)
+            @pl.when((l == 0) & (i == prep_at))
             def _():
-                chain(l, i)
-
-            intra(l, 2 * i)
-            intra(l, 2 * i + 1)
+                prep(1)
+
+            @pl.when((i >= lag) & (i < lag + HC))
+            def _():
+                chain(l, i - lag)
+
+            @pl.when(i < NT)
+            def _():
+                intra(l, i)
+
             return carry
 
-        lax.fori_loop(0, HALF, b_step, 0)
-
-        @pl.when(l == 0)
-        def _():
-            prep(1)
-
-        def c_step(i, carry):
-            @pl.when(jnp.logical_not(early))
-            def _():
-                chain(l, i)
-
-            return carry
-
-        lax.fori_loop(0, HALF, c_step, 0)
+        lax.fori_loop(0, 2 * NT, b_step, 0)
 
         sq[...] = jnp.zeros((TOK, 128), F32)
 
         def d_step(i, carry):
             @pl.when(i >= HALF)
             def _():
-                x_arrival(l, i - HALF).wait_recv()
+                x_arrival(l, 2 * (i - HALF)).wait_recv()
+                x_arrival(l, 2 * (i - HALF) + 1).wait_recv()
 
             tile = lax.rem(i + HALF * k, NT)
             cols = pl.ds(pl.multiple_of(tile * TILE, TILE), TILE)
@@ -531,16 +573,27 @@
             def _():
                 halo_copy(1).start()
 
-            @pl.when(l == LAYERS - 1)
+            for n in range(ROUND):
+
+                @pl.when((l == LAYERS - 1) & (i == n))
+                def _():
+                    round_copy(n, 0).start()
+
+            @pl.when((l == LAYERS - 1) & (i >= ROUND))
             def _():
                 o_copy(i).start()
 
             return carry
 
-        lax.fori_loop(0, TOK // 32, e_step, 0)
+        lax.fori_loop(0, RC, e_step, 0)
         return carry
 
     lax.fori_loop(0, LAYERS, layer, 0)
+
+    for hop in range(1, n_sec - 1):
+        for n in range(ROUND):
+            round_copy(n, hop - 1).wait_recv()
+            round_copy(n, hop).start()
 
     @pl.when(c + 1 < n_ctx)
     def _():
@@ -550,8 +603,12 @@
             halo_copy(l).wait_send()
 
     def sent(n, carry):
-        l, i = n // HALF, lax.rem(n, HALF)
-        l_copy(l, i).wait_send()
+        l, i = lax.div(n, HC), lax.rem(n, HC)
+
+        @pl.when(lax.rem(i, 2) == 0)
+        def _():
+            l_copy(l, lax.div(i, 2)).wait_send()
+
         x_copy(l, i).wait_send()
 
         @pl.when(z < last_z)
@@ -560,7 +617,7 @@
 
         return carry
 
-    lax.fori_loop(0, LAYERS * HALF, sent, 0)
+    lax.fori_loop(0, LAYERS * HC, sent, 0)
     for l in range(LAYERS):
         for d in range(1, n_tp):
             p_copy(l, d).wait_send()
@@ -570,21 +627,46 @@
         o_copy(i).wait_recv()
         return carry
 
-    lax.fori_loop(0, TOK // 32, moved, 0)
+    lax.fori_loop(ROUND, RC, moved, 0)
+    for n in range(ROUND):
+        for hop in range(n_sec - 1):
+            round_copy(n, hop).wait_send()
+        round_copy(n, n_sec - 2).wait_recv()
+
+
+def hand_over(made, out, rows, sem):
+    def part(n, way):
+        at = pl.ds(32 * n, 32)
+        if way == 0:
+            return pltpu.make_async_copy(made.at[0, at], rows.at[at], sem.at[0, n])
+        return pltpu.make_async_copy(rows.at[at], out.at[0, at], sem.at[1, n])
+
+    for n in range(RC):
+        part(n, 0).start()
+    for n in range(RC):
+        part(n, 0).wait()
+        part(n, 1).start()
+    for n in range(RC):
+        part(n, 1).wait()
 
 
 def per_device(sizes, *args):
-    hbm = pl.BlockSpec(memory_space=pl.ANY)
-    vmem = pl.BlockSpec(memory_space=pltpu.VMEM)
-    smem = pl.BlockSpec(memory_space=pltpu.SMEM)
+    hbm = pl.BlockSpec(memory_space=pltpu.HBM)
     dma = pltpu.SemaphoreType.DMA
-    n_tp = sizes[2]
-    return pl.pallas_call(
+    n_sec, _, n_tp = sizes
+    made = pl.pallas_call(
         functools.partial(kernel, *sizes),
         out_shape=jax.ShapeDtypeStruct((1, TOK, CH), BF16),
-        in_specs=[hbm, hbm, hbm, vmem, vmem, vmem, vmem, vmem, smem, vmem],
+        in_specs=[hbm] * len(args),
         out_specs=hbm,
         scratch_shapes=[
+            pltpu.VMEM((1, LAYERS, 32, TOK), F32),
+            pltpu.VMEM((1, LAYERS, 32, TOK), F32),
+            pltpu.VMEM((1, TOK), jnp.int32),
+            pltpu.VMEM((1, LAYERS, 4, CH), F32),
+            pltpu.VMEM((1, LAYERS, 4, 2, 128), F32),
+            pltpu.SMEM((1, LAYERS, 32), F32),
+            pltpu.VMEM((1, LAYERS, CH), F32),
             pltpu.VMEM((LAYERS + 1, BLK + TOK, CH), BF16),
             pltpu.VMEM((LAYERS, BLK + TOK, 256), BF16),
             pltpu.VMEM((1, TOK), jnp.int32),
@@ -605,33 +687,44 @@
             pltpu.VMEM((NT, 128, TILE), BF16),
             pltpu.VMEM((LAYERS, NT, 144, TILE), BF16),
             pltpu.VMEM((LAYERS, HALF, 144, TILE), BF16),
-            pltpu.VMEM((LAYERS, HALF, 128, TILE), BF16),
-            pltpu.VMEM((LAYERS, HALF, 128, TILE), BF16),
+            pltpu.VMEM((LAYERS, HC, 128, 128), BF16),
+            pltpu.VMEM((LAYERS, HC, 128, 128), BF16),
             pltpu.VMEM((LAYERS, NT, 128, TILE), BF16),
-            pltpu.VMEM((LAYERS, HALF, 128, TILE), BF16),
+            pltpu.VMEM((LAYERS, HC, 128, 128), BF16),
             pltpu.VMEM((TOK, CH), F32),
             pltpu.VMEM((TOK, CH), F32),
             pltpu.VMEM((TOK, 128), F32),
             pltpu.VMEM((LAYERS, 8, TOK), F32),
             pltpu.VMEM((LAYERS, max(n_tp - 1, 1), 8, TOK), F32),
             pltpu.VMEM((TOK, 128), F32),
-            dma((7,)),
+            dma((14,)),
             dma((2, LAYERS)),
             dma((2, 2)),
             dma((2, LAYERS, HALF)),
-            dma((2, LAYERS, HALF)),
-            dma((2, LAYERS, HALF)),
+            dma((2, LAYERS, HC)),
+            dma((2, LAYERS, HC)),
             dma((2, LAYERS, max(n_tp - 1, 1))),
-            dma((2, TOK // 32)),
+            dma((2, RC)),
+            dma((2, n_sec - 1, ROUND)),
+            pltpu.VMEM((max(n_sec - 2, 1), ROUND, 32, CH), BF16),
         ],
         compiler_params=pltpu.CompilerParams(
-            collective_id=0, has_side_effects=True, vmem_limit_bytes=48 * 1024 * 1024
+            collective_id=0, has_side_effects=True, vmem_limit_bytes=60 * 1024 * 1024
         ),
         cost_estimate=pl.CostEstimate(
             flops=2_000_000_000, bytes_accessed=6_000_000, transcendentals=6_000_000
         ),
         name="mixer",
     )(*args)
+    return pl.pallas_call(
+        hand_over,
+        out_shape=jax.ShapeDtypeStruct((1, TOK, CH), BF16),
+        in_specs=[pl.BlockSpec(memory_space=pl.ANY)],
+        out_specs=pl.BlockSpec(memory_space=pl.ANY),
+        scratch_shapes=[pltpu.VMEM((TOK, CH), BF16), dma((2, RC))],
+        name="hand_over",
+        compiler_params=pltpu.CompilerParams(vmem_limit_bytes=60 * 1024 * 1024),
+    )(made)
 
 
 def solution(mesh):

time: 96.6 us -> 80.6 us (0.83)
  local copies, waits for them, and re-layouts: 10 us -> 0 us
  Pallas kernels: 86.1 us -> 80.5 us
    unnamed x21 -> x0, local copies, waits for them, and re-layouts: 10 us -> none
    pallas_call x1, Pallas kernels: 86.1 us -> 78.4 us  [per_device(): pl.pallas_call(functools.partial(kernel, *sizes), out_shape=jax.ShapeDtyp...]
    pallas_call x0 -> x1, Pallas kernels: none -> 2.09 us  [per_device(): pl.pallas_call(hand_over, out_shape=jax.ShapeDtypeStruct((1, TOK, CH), BF...]
where the time goes in v2:
time: 80.6 us; the launch traced here: 80.5 us
  Pallas kernels  80.5 us (100%)
    pallas_call x1, Pallas kernels, per_device(): pl.pallas_call(functools.partial(kernel, *sizes), out_shape=jax.ShapeDtyp...  78.4 us
    pallas_call x1, Pallas kernels, per_device(): pl.pallas_call(hand_over, out_shape=jax.ShapeDtypeStruct((1, TOK, CH), BF...  2.09 us

profile of v2, /device:TPU:224, one launch (start us, length us, event | category | flops | bytes accessed | tf_op | source)
XLA Modules:
  0.0 80.5 jit_solution(4876709576669009716)
XLA Ops:
  0.0 78.4 %mixer.1.made = bf16[1,256,2048]{2,1,0:T(8,128)(2,1)} custom-call(bf16[1,256,2048]{2,1,0:T(8,128)(2,1)} %hid.1, bf16[1,2,256,2048]{3,2,1,0:T(8,128)(2,1)} %gate.1, bf16[1,2,2,256,128]{4,3,2,1,0:T(8,128)(2,1)} %proj.1, f32[1,2,32,256]{3,2,1,0:T(8,128)} %step_h.1, f32[1,2,32,256]{3,2,1,0:T(8,128)} %decay_h.1, s32[1,256]{1,0:T(1,128)} %ids_h.1, ...), custom_call_target="tpu_custom_call" | custom-call | flops 2000000000 | bytes 6000000 | tf_op jit(solution)/shard_map/mixer/pallas_call | solution.py:657
  78.4 2.1 %hand_over.1 = bf16[1,256,2048]{2,1,0:T(8,128)(2,1)} custom-call(bf16[1,256,2048]{2,1,0:T(8,128)(2,1)} %mixer.1.made), custom_call_target="tpu_custom_call" | custom-call | tf_op jit(solution)/shard_map/hand_over/pallas_call | solution.py:719

commit v3 on v2

--- a/solution.py
+++ b/solution.py
@@ -76,11 +76,11 @@
     pext,
     idp,
     gbuf,
-    mshift,
+    same_s,
     e2a,
     e2b,
-    e128,
-    cts,
+    ctf,
+    cum_f,
     va,
     vb,
     cum_s,
@@ -191,9 +191,6 @@
     head = iota((128, CH), 1) // HDIM
     e2a[...] = jnp.where((q < 64) & (q % 32 == head), 1.0, 0.0).astype(BF16)
     e2b[...] = jnp.where((q >= 64) & (q % 32 == head), 1.0, 0.0).astype(BF16)
-    q = iota((128, 4096), 0)
-    head = iota((128, 4096), 1) // 128
-    e128[...] = jnp.where((q < 96) & (q % 32 == head), 1.0, 0.0).astype(BF16)
     for l in range(LAYERS):
         uext[l, pl.ds(0, 112), :] = jnp.zeros((112, CH), BF16)
         pext[l, pl.ds(0, 112), :] = jnp.zeros((112, 256), BF16)
@@ -245,43 +242,66 @@
             cp.start()
         halo_copy(0).start()
 
+    m_row = ids[...].astype(F32)
+    m_e0 = m_row[:, 127:128]
+    m_e1 = m_row[:, 255:256]
+    lane = iota((32, TOK), 1)
+
+    def prep_decay(l):
+        d3 = jnp.concatenate(parts(decay[0, l], 3), axis=0).astype(BF16)
+        tri = jnp.where(iota((TOK, TOK), 0) <= iota((TOK, TOK), 1), 1.0, 0.0).astype(BF16)
+        c3 = mm(d3, tri)
+        cum = c3[0:32] + c3[32:64] + c3[64:96]
+        for j in range(NT):
+            cum_s[l, j, 0:4, :] = cum[4 * j : 4 * j + 4]
+        cum_f[l] = cum
+        cols = jnp.concatenate([cum, jnp.zeros((96, TOK), F32)], axis=0).T
+        for j in range(NT):
+            ctf[l, j] = pltpu.roll(cols, (128 - 4 * j) % 128, 1) if j else cols
+        tot0 = cum[:, 127:128]
+        tot1 = cum[:, 255:256]
+        first = lane < BLK
+        m_e = jnp.where(first[0:1], m_e0, m_e1)
+        tail = jnp.where(first, tot0, tot1) - cum
+        dt = step[0, l]
+        w = dt * jnp.where(m_row == m_e, jnp.exp(jnp.minimum(tail, 0.0)), 0.0)
+        va[l] = jnp.concatenate(parts(dt, 2) + parts(w, 2), axis=0).T.astype(BF16)
+
+    prep_decay(0)
+
     @pl.when(c >= 1)
     def _():
         for cp in first_copies():
             cp.wait_recv()
 
-    m_row = ids[...].astype(F32)
     m_old = idp[...].astype(F32)
     m_ext = jnp.concatenate([m_old[:, 128:], m_row], axis=1)
     m_prev = m_old[:, 255:256]
-    m_e0 = m_row[:, 127:128]
-    m_e1 = m_row[:, 255:256]
     m_col = jnp.broadcast_to(m_row, (128, TOK)).T
-    for b in range(2):
-        mine = m_col[b * BLK : (b + 1) * BLK]
-        mine = jnp.concatenate([mine, mine], axis=1)
-        same = mine == m_ext[:, b * BLK : b * BLK + 256]
-        gap = iota((BLK, 256), 0) + BLK - iota((BLK, 256), 1)
+    m_ext = jnp.broadcast_to(m_ext, (8, BLK + TOK))
+    for j in range(3):
+        back = pltpu.roll(m_ext, j + 1, 1)[0:1, BLK:]
+        same = jnp.where(back == m_row, 1.0, 0.0)
+        same_s[j] = jnp.broadcast_to(same, (128, TOK)).T
+
+
+    def conv(u, b, taps):
+        h = taps[3] * u[16:]
         for j in range(3):
-            mshift[b, pl.ds(j * BLK, BLK), :] = jnp.where(same & (gap == j + 1), 1.0, 0.0).astype(
-                BF16
-            )
-
-    lane = iota((32, TOK), 1)
+            same = same_s[j, pl.ds(b * BLK, BLK), :]
+            same = jnp.concatenate([same, same], axis=1)
+            h = h + taps[2 - j] * (same * pltpu.roll(u, j + 1, 0)[16:])
+        return h
 
     def prep(l):
         for b in range(2):
             rows = pl.ds(b * BLK, BLK)
-            moved = mm(mshift[b], pext[l, pl.ds(b * BLK, 256), :])
-            now = pext[l, pl.ds((b + 1) * BLK, BLK), :].astype(F32)
+            u = pext[l, pl.ds(b * BLK + 112, BLK + 16), :].astype(F32)
             taps = [
                 0.5 * jnp.concatenate([sw[0, l, t, 0:1, :], sw[0, l, t, 1:2, :]], axis=1)
                 for t in range(4)
             ]
-            h = taps[3] * now
-            for j in range(3):
-                h = h + taps[2 - j] * moved[j * BLK : (j + 1) * BLK]
-            v = silu_of_half(h)
+            v = silu_of_half(conv(u, b, taps))
             bm = v[:, :128]
             cm = v[:, 128:].astype(BF16)
             cmat_s[l, rows, :] = cm
@@ -291,22 +311,9 @@
                 m_col[b * BLK : (b + 1) * BLK] == m_row[:, b * BLK : (b + 1) * BLK]
             )
             sc_s[l, b] = jnp.where(ok, scores, 0.0)
-        d3 = jnp.concatenate(parts(decay[0, l], 3), axis=0).astype(BF16)
-        tri = jnp.where(iota((TOK, TOK), 0) <= iota((TOK, TOK), 1), 1.0, 0.0).astype(BF16)
-        c3 = mm(d3, tri)
-        cum = c3[0:32] + c3[32:64] + c3[64:96]
-        for j in range(NT):
-            cum_s[l, j, 0:4, :] = cum[4 * j : 4 * j + 4]
-        zero = jnp.zeros((32, TOK), F32)
-        cts[l] = jnp.concatenate(parts(cum, 3) + [zero], axis=0).T.astype(BF16)
+        cum = cum_f[l]
         tot0 = cum[:, 127:128]
-        tot1 = cum[:, 255:256]
         first = lane < BLK
-        m_e = jnp.where(first[0:1], m_e0, m_e1)
-        tail = jnp.where(first, tot0, tot1) - cum
-        dt = step[0, l]
-        w = dt * jnp.where(m_row == m_e, jnp.exp(jnp.minimum(tail, 0.0)), 0.0)
-        va[l] = jnp.concatenate(parts(dt, 2) + parts(w, 2), axis=0).T.astype(BF16)
         f = jnp.where(m_row == m_prev, jnp.exp(jnp.minimum(cum, 0.0)), 0.0)
         f1 = jnp.where(
             (m_row == m_e0) & jnp.logical_not(first), jnp.exp(jnp.minimum(cum - tot0, 0.0)), 0.0
@@ -398,11 +405,8 @@
         sums = []
         for b in range(2):
             rows = pl.ds(b * BLK, BLK)
-            moved = mm(mshift[b], uext[l, pl.ds(b * BLK, 256), cols])
-            h = taps[3] * uext[l, pl.ds((b + 1) * BLK, BLK), cols].astype(F32)
-            for j in range(3):
-                h = h + taps[2 - j] * moved[j * BLK : (j + 1) * BLK]
-            xs = silu_of_half(h).astype(BF16)
+            u = uext[l, pl.ds(b * BLK + 112, BLK + 16), cols].astype(F32)
+            xs = silu_of_half(conv(u, b, taps)).astype(BF16)
             xs_s[rows, cols] = xs
             xs = xs.astype(F32)
             v = va[l, rows, :]
@@ -458,17 +462,15 @@
         for b in range(2):
             rows = pl.ds(b * BLK, BLK)
             scores = sc_s[l, b]
+            decays = ctf[l, tile, rows, :]
             ys = []
             for p in range(2):
                 h0 = 4 * tile + 2 * p
                 pair = pl.ds(pl.multiple_of(tile * TILE + p * 128, 128), 128)
-                ct = mm(
-                    cts[l, rows, :],
-                    e128[:, pl.ds(pl.multiple_of(tile * 512 + p * 256, 256), 256)],
-                )
                 mix = []
                 for o in range(2):
-                    gap = ct[:, o * 128 : (o + 1) * 128] - cum_s[l, tile, 2 * p + o : 2 * p + o + 1, rows]
+                    q = 2 * p + o
+                    gap = decays[:, q : q + 1] - cum_s[l, tile, 2 * p + o : 2 * p + o + 1, rows]
                     mix.append((scores * jnp.exp(jnp.minimum(gap, 0.0))).astype(BF16))
                 dx = dx_s[rows, pair].astype(F32)
                 both = jnp.concatenate(
@@ -513,6 +515,7 @@
         def b_step(i, carry):
             @pl.when((l == 0) & (i == prep_at))
             def _():
+                prep_decay(1)
                 prep(1)
 
             @pl.when((i >= lag) & (i < lag + HC))
@@ -671,11 +674,11 @@
             pltpu.VMEM((LAYERS, BLK + TOK, 256), BF16),
             pltpu.VMEM((1, TOK), jnp.int32),
             pltpu.VMEM((LAYERS, TOK, CH), BF16),
-            pltpu.VMEM((2, 3 * BLK, 256), BF16),
+            pltpu.VMEM((3, TOK, 128), F32),
             pltpu.VMEM((128, CH), BF16),
             pltpu.VMEM((128, CH), BF16),
-            pltpu.VMEM((128, 4096), BF16),
-            pltpu.VMEM((LAYERS, TOK, 128), BF16),
+            pltpu.VMEM((LAYERS, NT, TOK, 128), F32),
+            pltpu.VMEM((LAYERS, 32, TOK), F32),
             pltpu.VMEM((LAYERS, TOK, 128), BF16),
             pltpu.VMEM((LAYERS, TOK, 128), BF16),
             pltpu.VMEM((LAYERS, NT, 8, TOK), F32),

time: 80.6 us -> 76.6 us (0.950)
  Pallas kernels: 80.5 us -> 76.5 us
    pallas_call x1, Pallas kernels: 78.4 us -> 74.4 us  [per_device(): pl.pallas_call(functools.partial(kernel, *sizes), out_shape=jax.ShapeDtyp...]
where the time goes in v3:
time: 76.6 us; the launch traced here: 76.5 us
  Pallas kernels  76.5 us (100%)
    pallas_call x1, Pallas kernels, per_device(): pl.pallas_call(functools.partial(kernel, *sizes), out_shape=jax.ShapeDtyp...  74.4 us
    pallas_call x1, Pallas kernels, per_device(): pl.pallas_call(hand_over, out_shape=jax.ShapeDtypeStruct((1, TOK, CH), BF...  2.09 us

profile of v3, /device:TPU:224, one launch (start us, length us, event | category | flops | bytes accessed | tf_op | source)
XLA Modules:
  0.0 76.5 jit_solution(16613825108717666412)
XLA Ops:
  0.0 74.4 %mixer.1.made = bf16[1,256,2048]{2,1,0:T(8,128)(2,1)} custom-call(bf16[1,256,2048]{2,1,0:T(8,128)(2,1)} %hid.1, bf16[1,2,256,2048]{3,2,1,0:T(8,128)(2,1)} %gate.1, bf16[1,2,2,256,128]{4,3,2,1,0:T(8,128)(2,1)} %proj.1, f32[1,2,32,256]{3,2,1,0:T(8,128)} %step_h.1, f32[1,2,32,256]{3,2,1,0:T(8,128)} %decay_h.1, s32[1,256]{1,0:T(1,128)} %ids_h.1, ...), custom_call_target="tpu_custom_call" | custom-call | flops 2000000000 | bytes 6000000 | tf_op jit(solution)/shard_map/mixer/pallas_call | solution.py:660
  74.4 2.1 %hand_over.1 = bf16[1,256,2048]{2,1,0:T(8,128)(2,1)} custom-call(bf16[1,256,2048]{2,1,0:T(8,128)(2,1)} %mixer.1.made), custom_call_target="tpu_custom_call" | custom-call | tf_op jit(solution)/shard_map/hand_over/pallas_call | solution.py:722

commit v4 on v3

--- a/solution.py
+++ b/solution.py
@@ -17,6 +17,7 @@
 HC = 2 * HALF
 RC = TOK // 32
 ROUND = RC // 4
+PART = CH // 2
 LAG = 4
 LAYERS = 2
 F32 = jnp.float32
@@ -112,6 +113,15 @@
     o_sem,
     r_sem,
     relay,
+    e_sem,
+    out_sem,
+    u_r,
+    scale_s,
+    scale_r,
+    gated_s,
+    gated_r,
+    g_sem,
+    relay_g,
 ):
     sec = lax.axis_index("section")
     c = lax.axis_index("ctx")
@@ -121,6 +131,8 @@
     last_z = n_ctx // 2 - 1
     partner = c + 1 - 2 * k
     core0 = k == 0
+    ahead = pl.ds(pl.multiple_of(k * PART, PART), PART)
+    late = pl.ds(pl.multiple_of((1 - k) * PART, PART), PART)
 
     in_small = []
     for n, (src, dst) in enumerate(
@@ -378,8 +390,8 @@
     def o_copy(i):
         row = TOK - 32 * (i + 1)
         return pltpu.make_async_remote_copy(
-            src_ref=uext.at[LAYERS, pl.ds(pl.multiple_of(BLK + row, 32), 32)],
-            dst_ref=out.at[0, pl.ds(pl.multiple_of(row, 32), 32)],
+            src_ref=uext.at[LAYERS, pl.ds(pl.multiple_of(BLK + row, 32), 32), late],
+            dst_ref=out.at[0, pl.ds(pl.multiple_of(row, 32), 32), late],
             send_sem=o_sem.at[0, i],
             recv_sem=o_sem.at[1, i],
             device_id={"section": lax.rem(sec + 1, n_sec)},
@@ -389,10 +401,39 @@
     def round_copy(i, hop):
         row = TOK - 32 * (i + 1)
         return pltpu.make_async_remote_copy(
-            src_ref=uext.at[LAYERS, pl.ds(BLK + row, 32)] if hop == 0 else relay.at[hop - 1, i],
-            dst_ref=out.at[0, pl.ds(row, 32)] if hop == n_sec - 2 else relay.at[hop, i],
+            src_ref=uext.at[LAYERS, pl.ds(BLK + row, 32), late] if hop == 0 else relay.at[hop - 1, i],
+            dst_ref=out.at[0, pl.ds(row, 32), late] if hop == n_sec - 2 else relay.at[hop, i],
             send_sem=r_sem.at[0, hop, i],
             recv_sem=r_sem.at[1, hop, i],
+            device_id={"section": lax.rem(sec + n_sec - 1, n_sec)},
+            device_id_type=MESH,
+        )
+
+    def next_copy(src, dst, n):
+        return pltpu.make_async_remote_copy(
+            src_ref=src,
+            dst_ref=dst,
+            send_sem=e_sem.at[0, n],
+            recv_sem=e_sem.at[1, n],
+            device_id={"section": lax.rem(sec + 1, n_sec)},
+            device_id_type=MESH,
+        )
+
+    def stream_copy():
+        return next_copy(uext.at[LAYERS - 1, pl.ds(BLK, TOK), ahead], u_r, 0)
+
+    def scale_copy():
+        return next_copy(scale_s, scale_r, 1)
+
+    def gated_copy(i):
+        return next_copy(gated_s.at[i], gated_r.at[i], 2 + i)
+
+    def gated_round(hop):
+        return pltpu.make_async_remote_copy(
+            src_ref=gated_s.at[0] if hop == 0 else relay_g.at[hop - 1],
+            dst_ref=gated_r.at[0] if hop == n_sec - 2 else relay_g.at[hop],
+            send_sem=g_sem.at[0, hop],
+            recv_sem=g_sem.at[1, hop],
             device_id={"section": lax.rem(sec + n_sec - 1, n_sec)},
             device_id_type=MESH,
         )
@@ -493,6 +534,10 @@
         def _():
             halo_copy(l).wait_recv()
 
+        @pl.when(l == LAYERS - 1)
+        def _():
+            stream_copy().start()
+
         def a_step(i, carry):
             local_part(l, i)
 
@@ -542,6 +587,19 @@
             cols = pl.ds(pl.multiple_of(tile * TILE, TILE), TILE)
             g = g1[:, cols] + g2[:, cols] * mm(cmat_s[l], x_s[l, tile])
             g1[:, cols] = g
+
+            @pl.when((l == LAYERS - 1) & (i < HALF))
+            def _():
+                gated_s[i] = (g * gain[0, LAYERS - 1 : LAYERS, cols]).astype(BF16)
+
+                @pl.when(i == 0)
+                def _():
+                    gated_round(0).start()
+
+                @pl.when(i > 0)
+                def _():
+                    gated_copy(i).start()
+
             g = g * g
             sq[...] += g[:, :128] + g[:, 128:]
             return carry
@@ -560,17 +618,30 @@
         scale = lax.rsqrt(total[0:1] / (CH * n_tp) + 1e-05)
         r_s[...] = jnp.broadcast_to(scale, (128, TOK)).T
 
+        @pl.when(l == LAYERS - 1)
+        def _():
+            scale_s[...] = jnp.broadcast_to(scale, (8, TOK))
+            scale_copy().start()
+
         def e_step(i, carry):
             row = TOK - 32 * (i + 1)
             rows = pl.ds(pl.multiple_of(row, 32), 32)
             ext = pl.ds(pl.multiple_of(BLK + row, 32), 32)
             r = r_s[rows, :]
-            for t in range(CH // 128):
-                cols = pl.ds(t * 128, 128)
-                gains = jnp.where(l == 0, gain[0, 0:1, cols], gain[0, 1:2, cols])
-                uext[l + 1, ext, cols] = (
-                    uext[l, ext, cols].astype(F32) + g1[rows, cols] * (gains * r)
-                ).astype(BF16)
+
+            def rows_of(start):
+                for t in range(PART // 128):
+                    cols = pl.ds(pl.multiple_of(start * PART + t * 128, 128), 128)
+                    gains = jnp.where(l == 0, gain[0, 0:1, cols], gain[0, 1:2, cols])
+                    uext[l + 1, ext, cols] = (
+                        uext[l, ext, cols].astype(F32) + g1[rows, cols] * (gains * r)
+                    ).astype(BF16)
+
+            rows_of(1 - k)
+
+            @pl.when(l < LAYERS - 1)
+            def _():
+                rows_of(k)
 
             @pl.when((l == 0) & (i == 0) & (c + 1 < n_ctx))
             def _():
@@ -594,9 +665,27 @@
     lax.fori_loop(0, LAYERS, layer, 0)
 
     for hop in range(1, n_sec - 1):
+        gated_round(hop - 1).wait_recv()
+        gated_round(hop).start()
         for n in range(ROUND):
             round_copy(n, hop - 1).wait_recv()
             round_copy(n, hop).start()
+
+    stream_copy().wait_recv()
+    scale_copy().wait_recv()
+    scale_col = jnp.broadcast_to(scale_r[0:1, :], (128, TOK)).T
+    scale_col = jnp.concatenate([scale_col, scale_col], axis=1)
+
+    def own_out(i):
+        at = pl.ds(pl.multiple_of(k * PART + i * TILE, TILE), TILE)
+        return pltpu.make_async_copy(gated_r.at[i], out.at[0, :, at], out_sem.at[i])
+
+    for i in (1, 2, 3, 0):
+        (gated_copy(i) if i else gated_round(n_sec - 2)).wait_recv()
+        gated_r[i] = (
+            u_r[:, i * TILE : (i + 1) * TILE].astype(F32) + gated_r[i].astype(F32) * scale_col
+        ).astype(BF16)
+        own_out(i).start()
 
     @pl.when(c + 1 < n_ctx)
     def _():
@@ -631,6 +720,14 @@
         return carry
 
     lax.fori_loop(ROUND, RC, moved, 0)
+    stream_copy().wait_send()
+    scale_copy().wait_send()
+    for hop in range(n_sec - 1):
+        gated_round(hop).wait_send()
+    for i in range(HALF):
+        own_out(i).wait()
+        if i:
+            gated_copy(i).wait_send()
     for n in range(ROUND):
         for hop in range(n_sec - 1):
             round_copy(n, hop).wait_send()
@@ -709,7 +806,16 @@
             dma((2, LAYERS, max(n_tp - 1, 1))),
             dma((2, RC)),
             dma((2, n_sec - 1, ROUND)),
-            pltpu.VMEM((max(n_sec - 2, 1), ROUND, 32, CH), BF16),
+            pltpu.VMEM((max(n_sec - 2, 1), ROUND, 32, PART), BF16),
+            dma((2, 2 + HALF)),
+            dma((HALF,)),
+            pltpu.VMEM((TOK, PART), BF16),
+            pltpu.VMEM((8, TOK), F32),
+            pltpu.VMEM((8, TOK), F32),
+            pltpu.VMEM((HALF, TOK, TILE), BF16),
+            pltpu.VMEM((HALF, TOK, TILE), BF16),
+            dma((2, n_sec - 1)),
+            pltpu.VMEM((max(n_sec - 2, 1), TOK, TILE), BF16),
         ],
         compiler_params=pltpu.CompilerParams(
             collective_id=0, has_side_effects=True, vmem_limit_bytes=60 * 1024 * 1024

time: 76.6 us -> 74 us (0.966)
  Pallas kernels: 76.5 us -> 73.8 us
    pallas_call x1, Pallas kernels: 74.4 us -> 71.7 us  [per_device(): pl.pallas_call(functools.partial(kernel, *sizes), out_shape=jax.ShapeDtyp...]
where the time goes in v4:
time: 74 us; the launch traced here: 73.8 us
  Pallas kernels  73.8 us (100%)
    pallas_call x1, Pallas kernels, per_device(): pl.pallas_call(functools.partial(kernel, *sizes), out_shape=jax.ShapeDtyp...  71.7 us
    pallas_call x1, Pallas kernels, per_device(): pl.pallas_call(hand_over, out_shape=jax.ShapeDtypeStruct((1, TOK, CH), BF...  2.09 us

profile of v4, /device:TPU:224, one launch (start us, length us, event | category | flops | bytes accessed | tf_op | source)
XLA Modules:
  0.0 73.8 jit_solution(17285512741389976746)
XLA Ops:
  0.0 71.7 %mixer.1.made = bf16[1,256,2048]{2,1,0:T(8,128)(2,1)} custom-call(bf16[1,256,2048]{2,1,0:T(8,128)(2,1)} %hid.1, bf16[1,2,256,2048]{3,2,1,0:T(8,128)(2,1)} %gate.1, bf16[1,2,2,256,128]{4,3,2,1,0:T(8,128)(2,1)} %proj.1, f32[1,2,32,256]{3,2,1,0:T(8,128)} %step_h.1, f32[1,2,32,256]{3,2,1,0:T(8,128)} %decay_h.1, s32[1,256]{1,0:T(1,128)} %ids_h.1, ...), custom_call_target="tpu_custom_call" | custom-call | flops 2000000000 | bytes 6000000 | tf_op jit(solution)/shard_map/mixer/pallas_call | solution.py:757
  71.7 2.1 %hand_over.1 = bf16[1,256,2048]{2,1,0:T(8,128)(2,1)} custom-call(bf16[1,256,2048]{2,1,0:T(8,128)(2,1)} %mixer.1.made), custom_call_target="tpu_custom_call" | custom-call | tf_op jit(solution)/shard_map/hand_over/pallas_call | solution.py:828
